TPU v7x, 32 devices: a whole 2x2x4 slice. The times are simulated.
32 devices in a mesh: seq: 8 (over z, core), tp: 4 (over y, x).
Axes of the slice: x: 2, y: 2, z: 4, core: 2. Of those that a mesh axis runs over, the one named last changes fastest.
Arguments:
- tokens: bfloat16 [4, 1024, 4096], P(None, 'seq', 'tp'), may hold values from -6 to 6
- new_tokens: bfloat16 [4, 4096], P(None, 'tp'), may hold values from -6 to 6
- w_qkv: bfloat16 [3, 4096, 4096], P(None, None, 'tp')
- w_out: bfloat16 [4096, 4096], P('tp')
- q_gain: float32 [4096], P('tp'), may hold values from 0.5 to 6
- k_gain: float32 [4096], P('tp'), may hold values from 0.5 to 6
- post_gain: float32 [4096], P('tp'), may hold values from 0.5 to 1.5
- lengths: int32 [4], replicated, may hold values from 1 to 1024, 3072 in all
Outputs:
- hidden_out: bfloat16 [4, 1024, 4096], P(None, 'seq', 'tp')
- new_out: bfloat16 [4, 4096], P(None, 'tp')
Inputs may be any that keep to these rules, and one draw needn't show every extreme that they name: `lengths`: one prompt has exactly 1024 live tokens.
All inputs are finite; a program needn't handle non-finite values.
Results may differ from a plain program's by a relative error of at most 0.012.
The roundings to bfloat16 on the way count: a program that leaves them out, or rounds other values in their place, can miss the bound.
Values may be sent and summed in bfloat16 or wider, within the bound.
A program may use at most 128 MiB of HBM per device.

v0:
```python
from functools import partial

import jax
import jax.numpy as jnp
from jax import lax
from jax.sharding import PartitionSpec as P

HD = 128


rope_base = 500000.0
norm_eps = 1e-06
masked_fill = -1e30


def joined(value, axis, combine):
    everything = jax.tree.map(lambda part: lax.all_gather(part, axis), value)
    initial = jax.tree.map(lambda part: part[0], everything)

    def hop(k, so_far):
        return combine(so_far, jax.tree.map(lambda part: part[k], everything))

    return lax.fori_loop(1, lax.axis_size(axis), hop, initial)


def rotate(values, position):
    half = values.shape[-1] // 2
    freq = rope_base ** (-(jnp.arange(half, dtype=jnp.float32) * 2.0) / values.shape[-1])
    angle = position.astype(jnp.float32)[..., None] * freq
    cosine = jnp.cos(angle)
    sine = jnp.sin(angle)
    lower = values[..., :half]
    upper = values[..., half:]
    return jnp.concatenate([lower * cosine - upper * sine, upper * cosine + lower * sine], -1)


def fold_step(carry, pieces, start, queries, query_pos, lengths, scale):
    running_max, running_sum, running_acc = carry
    key_piece, value_piece = pieces
    count = key_piece.shape[1]
    scores = (
        jnp.einsum("sphe,snhe->shpn", queries, key_piece, preferred_element_type=jnp.float32)
        * scale
    )
    key_pos = jnp.arange(count, dtype=jnp.int32)
    valid = (key_pos[None, None, :] <= query_pos[None, :, None]) & (
        key_pos[None, None, :] < lengths[:, None, None]
    )
    valid = valid[:, None, :, :]
    scores = jnp.where(valid, scores, masked_fill)
    new_max = jnp.maximum(running_max, jnp.max(scores, -1))
    weights = jnp.where(valid, jnp.exp(scores - new_max[..., None]), 0.0)
    running_sum = jnp.sum(weights, -1)
    running_acc = jnp.einsum(
        "shpn,snhe->shpe",
        weights.astype(jnp.bfloat16),
        value_piece,
        preferred_element_type=jnp.float32,
    )
    return (new_max, running_sum, running_acc)


def combine(first, second):
    first_max, first_sum, first_acc = first
    second_max, second_sum, second_acc = second
    top = jnp.maximum(first_max, second_max)
    first_factor = jnp.exp(first_max - top)
    second_factor = jnp.exp(second_max - top)
    return (
        top,
        first_sum * first_factor + second_sum * second_factor,
        first_acc * first_factor[..., None] + second_acc * second_factor[..., None],
    )


def body(tokens, new_tokens, w_qkv, w_out, q_gain, k_gain, post_gain, lengths):
    seqs, pos_dev, width_local = tokens.shape
    heads_local = width_local // HD
    full_width = w_qkv.shape[1]
    prompt_rows = seqs * pos_dev
    flat_rows = tokens.reshape(prompt_rows, width_local)
    row_piece = lax.all_gather(flat_rows, "tp", axis=1, tiled=True)
    new_piece = lax.all_gather(new_tokens, "tp", axis=1, tiled=True)
    proj_rows = jnp.einsum("tn,cnf->ctf", row_piece, w_qkv, preferred_element_type=jnp.float32)
    proj_new = jnp.einsum("tn,cnf->ctf", new_piece, w_qkv, preferred_element_type=jnp.float32)
    query_rows, key_rows = (proj_rows[0], proj_rows[1])
    query_fresh, key_fresh = (proj_new[0], proj_new[1])
    query_sq, key_sq, query_new_sq, key_new_sq = lax.psum(
        (
            jnp.sum(query_rows * query_rows, -1),
            jnp.sum(key_rows * key_rows, -1),
            jnp.sum(query_fresh * query_fresh, -1),
            jnp.sum(key_fresh * key_fresh, -1),
        ),
        "tp",
    )

    def normed(values, square_sum, gain):
        return values * lax.rsqrt(square_sum[:, None] / full_width + norm_eps) * gain

    seq_index = lax.axis_index("seq")
    query_pos = seq_index * pos_dev + jnp.arange(pos_dev, dtype=jnp.int32)
    row_pos = jnp.tile(query_pos, seqs)
    queries = rotate(
        normed(query_rows, query_sq, q_gain).reshape(prompt_rows, heads_local, HD), row_pos[:, None]
    )
    queries = queries.astype(jnp.bfloat16).reshape(seqs, pos_dev, heads_local, HD)
    keys = rotate(
        normed(key_rows, key_sq, k_gain).reshape(prompt_rows, heads_local, HD), row_pos[:, None]
    )
    keys = keys.astype(jnp.bfloat16).reshape(seqs, pos_dev, heads_local, HD)
    values = proj_rows[2].astype(jnp.bfloat16).reshape(seqs, pos_dev, heads_local, HD)
    new_queries = rotate(
        normed(query_fresh, query_new_sq, q_gain).reshape(seqs, heads_local, HD), lengths[:, None]
    ).astype(jnp.bfloat16)
    new_keys = rotate(
        normed(key_fresh, key_new_sq, k_gain).reshape(seqs, heads_local, HD), lengths[:, None]
    ).astype(jnp.bfloat16)
    new_values = proj_new[2].astype(jnp.bfloat16).reshape(seqs, heads_local, HD)
    scale = HD ** (-0.5)
    start_carry = (
        jnp.full((seqs, heads_local, pos_dev), masked_fill, jnp.float32),
        jnp.zeros((seqs, heads_local, pos_dev), jnp.float32),
        jnp.zeros((seqs, heads_local, pos_dev, HD), jnp.float32),
    )
    stepper = partial(fold_step, queries=queries, query_pos=query_pos, lengths=lengths, scale=scale)
    final_max, final_sum, final_acc = stepper(
        start_carry,
        (
            lax.all_gather(keys, "seq", axis=1, tiled=True),
            lax.all_gather(values, "seq", axis=1, tiled=True),
        ),
        jnp.int32(0),
    )
    attention = (
        (final_acc / final_sum[..., None])
        .transpose(0, 2, 1, 3)
        .reshape(prompt_rows, width_local)
        .astype(jnp.bfloat16)
    )
    local_scores = (
        jnp.einsum("she,sphe->shp", new_queries, keys, preferred_element_type=jnp.float32) * scale
    )
    live = (query_pos[None, :] < lengths[:, None])[:, None, :]
    local_scores = jnp.where(live, local_scores, masked_fill)
    local_max = jnp.max(local_scores, -1)
    local_weights = jnp.where(live, jnp.exp(local_scores - local_max[..., None]), 0.0)
    local_sum = jnp.sum(local_weights, -1)
    local_acc = jnp.einsum(
        "shp,sphe->she",
        local_weights.astype(jnp.bfloat16),
        values,
        preferred_element_type=jnp.float32,
    )
    merged_max, merged_sum, merged_acc = joined((local_max, local_sum, local_acc), "seq", combine)
    self_score = (
        jnp.einsum("she,she->sh", new_queries, new_keys, preferred_element_type=jnp.float32) * scale
    )
    new_top = jnp.maximum(merged_max, self_score)
    keep_factor = jnp.exp(merged_max - new_top)
    own_weight = jnp.exp(self_score - new_top)
    new_total = merged_sum * keep_factor + own_weight
    own_rounded = lax.optimization_barrier(own_weight.astype(jnp.bfloat16)).astype(jnp.float32)
    numer = merged_acc * keep_factor[..., None] + own_rounded[..., None] * new_values.astype(
        jnp.float32
    )
    new_attention = (numer / new_total[..., None]).reshape(seqs, width_local).astype(jnp.bfloat16)
    part_rows = jnp.dot(attention, w_out, preferred_element_type=jnp.float32)
    part_new = jnp.dot(new_attention, w_out, preferred_element_type=jnp.float32)
    sum_rows, sum_new = (
        lax.psum(part_rows.astype(jnp.bfloat16), "tp").astype(jnp.float32),
        lax.psum(part_new.astype(jnp.bfloat16), "tp").astype(jnp.float32),
    )
    mean_rows = jnp.mean(sum_rows * sum_rows, -1)
    mean_new = jnp.mean(sum_new * sum_new, -1)
    offset = lax.axis_index("tp") * width_local
    own_rows = lax.dynamic_slice_in_dim(sum_rows, offset, width_local, 1)
    own_new = lax.dynamic_slice_in_dim(sum_new, offset, width_local, 1)
    out_rows = (
        flat_rows.astype(jnp.float32)
        + own_rows * lax.rsqrt(mean_rows[:, None] + norm_eps) * post_gain
    )
    out_new = (
        new_tokens.astype(jnp.float32)
        + own_new * lax.rsqrt(mean_new[:, None] + norm_eps) * post_gain
    )
    return (
        out_rows.astype(jnp.bfloat16).reshape(seqs, pos_dev, width_local),
        out_new.astype(jnp.bfloat16),
    )


def solution(mesh):
    in_specs = (
        P(None, "seq", "tp"),
        P(None, "tp"),
        P(None, None, "tp"),
        P("tp", None),
        P("tp"),
        P("tp"),
        P("tp"),
        P(),
    )
    out_specs = (P(None, "seq", "tp"), P(None, "tp"))
    return jax.shard_map(body, mesh=mesh, in_specs=in_specs, out_specs=out_specs, check_vma=False)
```

profile of v0, /device:TPU:0, one launch (start us, length us, event | category | flops | bytes accessed | tf_op | source)
XLA Modules:
  0.0 409.2 jit_solution(9443149900115329469)
XLA Ops:
  7.2 0.7 all-gather.9.cloned.1.call-update
  7.9 9.8 %all_gather.33 = bf16[4,4096]{1,0:T(4,128)(2,1)S(1)} all-gather(bf16[4,1024]{1,0:T(4,128)(2,1)} %param.11), channel_id=1, replica_groups=mesh['seq'=8,'tp'=4] {'tp'}, dimensions={1}, use_global_device_ids=true | all-gather | bytes 40960 | tf_op jit(solution)/shard_map/all_gather | solution.py:83
  17.7 11.0 %convolution_bitcast_fusion = f32[3,4,1024]{2,1,0:T(4,128)S(1)} fusion(bf16[3,4096,1024]{2,1,0:T(8,128)(2,1)} %param.12, bf16[4,4096]{1,0:T(4,128)(2,1)S(1)} %all_gather.33), kind=kOutput, calls=%fused_computation.33 | convolution fusion | flops 100663296 | bytes 25247744 | tf_op jit(solution)/shard_map/tn,cnf->ctf/dot_general | solution.py:85
  28.7 0.2 multiply_reduce_fusion.4
  28.9 0.5 multiply_cosine_fusion
  29.4 35.8 %all-gather.9.cloned.1.call-done = bf16[512,4096]{1,0:T(8,128)(2,1)} async-done(((bf16[512,1024]{1,0:T(8,128)(2,1)}), bf16[512,4096]{1,0:T(8,128)(2,1)}) %all-gather.9.cloned.1.call-update) | async-done | bytes 4194320 | tf_op jit(solution)/shard_map/all_gather | solution.py:82
  65.3 17.9 %fusion.15 = f32[3,512,1024]{1,2,0:T(8,128)S(1)} fusion(bf16[3,4096,1024]{2,1,0:T(8,128)(2,1)} %param.12, bf16[512,4096]{1,0:T(8,128)(2,1)} %all-gather.9.cloned.1.call-done), kind=kOutput, calls=%fused_computation.24 | convolution fusion | flops 12884901888 | bytes 35651584 | tf_op jit(solution)/shard_map/tn,cnf->ctf/dot_general | solution.py:84
  83.2 2.7 copy-done.1
  85.8 2.0 multiply_reduce_fusion.2
  87.8 9.0 %all-reduce = (f32[512]{0:T(512)S(1)}, f32[512]{0:T(512)S(1)}, f32[4]{0:T(128)S(1)}, f32[4]{0:T(128)S(1)}) all-reduce(f32[512]{0:T(512)S(1)} %get-tuple-element.184, f32[512]{0:T(512)S(1)} %get-tuple-element.183, f32[4]{0:T(128)S(1)} %get-tuple-element.186, f32[4]{0:T(128)S(1)} %get-tuple-element.185), channel_id=1, replica_groups=mesh['seq'=8,'tp'=4] {'tp'}, use_global_device_ids=true, to_apply=%region_3.0 | all-reduce | flops 1032 | bytes 8256 | tf_op jit(solution)/shard_map/psum | solution.py:88
  96.9 1.8 multiply_multiply_fusion
  98.7 0.2 multiply_multiply_fusion.1
  99.0 1.7 subtract_convert_fusion.1
  100.8 0.7 copy.22
  101.7 0.7 copy.23
  102.4 1.6 pad_maximum_fusion
  104.0 1.8 slice.120
  105.8 0.3 convert_element_type.91
  106.1 1.5 copy.24
  108.0 0.1 iota_compare_fusion
  108.1 0.2 broadcast_and_fusion
  108.6 0.7 fusion.36
  109.4 0.2 fusion.41
  109.5 1.7 fusion.34
  111.2 15.3 %all-gather.2 = f32[32,8,128]{2,1,0:T(8,128)S(1)} all-gather(f32[4,8,128]{2,1,0:T(8,128)S(1)} %bitcast.123), channel_id=4, replica_groups=mesh['seq'=8,'tp'=4] {'seq'}, dimensions={0}, use_global_device_ids=true | all-gather | bytes 147456 | tf_op jit(solution)/shard_map/all_gather | solution.py:17
  126.5 1.2 concatenate.26
  127.7 0.7 copy.20
  128.4 0.1 concatenate.27
  128.5 0.7 copy.21
  129.2 14.1 %all-gather.4 = f32[8,4,8]{2,1,0:T(4,128)S(1)} all-gather(f32[1,4,8]{2,1,0:T(4,128)S(1)} %bitcast.130), channel_id=3, replica_groups=mesh['seq'=8,'tp'=4] {'seq'}, dimensions={0}, use_global_device_ids=true | all-gather | bytes 1152 | tf_op jit(solution)/shard_map/all_gather | solution.py:17
  143.3 13.9 %all-gather.3 = f32[8,4,8]{2,1,0:T(4,128)S(1)} all-gather(f32[1,4,8]{2,1,0:T(4,128)S(1)} %bitcast.124), channel_id=2, replica_groups=mesh['seq'=8,'tp'=4] {'seq'}, dimensions={0}, use_global_device_ids=true | all-gather | bytes 1152 | tf_op jit(solution)/shard_map/all_gather | solution.py:17
  157.1 0.2 fusion.33
  157.3 30.0 %all-gather.11.cloned.1.call-done = bf16[4,1024,8,128]{3,1,2,0:T(8,128)(2,1)} async-done(((bf16[4,128,8,128]{3,1,2,0:T(8,128)(2,1)}), bf16[4,1024,8,128]{3,1,2,0:T(8,128)(2,1)}) %all-gather.11.cloned.1.call-update) | async-done | bytes 8388624 | tf_op jit(solution)/shard_map/all_gather | solution.py:130
  187.3 14.0 %fusion.3 = (f32[4,8,128]{2,1,0:T(8,128)S(1)}, f32[4,8,128,1024]{3,2,1,0:T(8,128)}) fusion(pred[4,128,1024]{2,1,0:T(8,128)(4,1)S(1)} %broadcast_and_fusion, bf16[4,1024,8,128]{3,1,2,0:T(8,128)(2,1)} %all-gather.11.cloned.1.call-done, bf16[4,128,8,64]{3,1,2,0:T(8,128)(2,1)S(1)} %copy.21, bf16[4,128,8,64]{3,1,2,0:T(8,128)(2,1)S(1)} %copy.20), kind=kOutput, calls=%fused_computation.10 | convolution fusion | flops 1088417792 | bytes 26755072 | tf_op jit(solution)/shard_map/sphe,snhe->shpn/dot_general | solution.py:42
  201.3 8.5 %fusion.4 = f32[4,8,128]{2,1,0:T(8,128)S(1)} fusion(f32[4,8,128,1024]{3,2,1,0:T(8,128)} %get-tuple-element.235, f32[4,8,128]{2,1,0:T(8,128)S(1)} %broadcast_maximum_fusion, pred[4,128,1024]{2,1,0:T(8,128)(4,1)S(1)} %broadcast_and_fusion), kind=kLoop, calls=%fused_computation.11 | loop fusion | flops 20967424 | bytes 17334272 | tf_op jit(solution)/shard_map/reduce_sum | solution.py:53
  209.9 60.0 %all-gather.13.cloned.1.call-done = bf16[4,1024,8,128]{3,1,2,0:T(8,128)(2,1)} async-done(((bf16[4,128,8,128]{3,1,2,0:T(8,128)(2,1)}), bf16[4,1024,8,128]{3,1,2,0:T(8,128)(2,1)}) %all-gather.13.cloned.1.call-update) | async-done | bytes 8388624 | tf_op jit(solution)/shard_map/all_gather | solution.py:131
  269.9 11.3 %fusion.18 = bf16[4,128,8,128]{3,1,2,0:T(8,128)(2,1)S(1)} fusion(bf16[4,1024,8,128]{3,1,2,0:T(8,128)(2,1)} %all-gather.13.cloned.1.call-done, f32[4,8,128,1024]{3,2,1,0:T(8,128)} %get-tuple-element.235, f32[4,8,128]{2,1,0:T(8,128)S(1)} %broadcast_maximum_fusion, pred[4,128,1024]{2,1,0:T(8,128)(4,1)S(1)} %broadcast_and_fusion, f32[4,128,8]{1,2,0:T(8,128)S(1)} %bitcast.129), kind=kOutput, calls=%fused_computation.27 | convolution fusion | flops 1095761920 | bytes 26771456 | tf_op jit(solution)/shard_map/shpn,snhe->shpe/dot_general | solution.py:54
  281.2 0.7 copy.25
  281.9 9.4 %convolution_convert_fusion = bf16[512,4096]{1,0:T(8,128)(2,1)} fusion(bf16[1024,4096]{1,0:T(8,128)(2,1)} %param.13, bf16[64,8,8,128]{3,2,1,0:T(8,128)(2,1)S(1)} %bitcast.119), kind=kOutput, calls=%fused_computation.20 | convolution fusion | flops 4297064448 | bytes 13631488 | tf_op jit(solution)/shard_map/dot_general | solution.py:168
  291.4 0.7 while.19
  292.2 4.7 %convolution_convert_fusion.1 = bf16[4,4096]{1,0:T(4,128)(2,1)S(1)} fusion(bf16[1024,4096]{1,0:T(8,128)(2,1)} %param.13, bf16[1,4,8,128]{3,2,1,0:T(8,128)(2,1)S(1)} %fusion.44), kind=kOutput, calls=%fused_computation.21 | convolution fusion | flops 33570816 | bytes 8429568 | tf_op jit(solution)/shard_map/dot_general | solution.py:169
  296.9 17.1 %psum.47 = bf16[4,4096]{1,0:T(4,128)(2,1)S(1)} all-reduce(bf16[4,4096]{1,0:T(4,128)(2,1)S(1)} %convolution_convert_fusion.1), channel_id=1, replica_groups=mesh['seq'=8,'tp'=4] {'tp'}, use_global_device_ids=true, to_apply=%region_16.17 | all-reduce | flops 16384 | bytes 65536 | tf_op jit(solution)/shard_map/psum | solution.py:172
  314.0 0.1 multiply_reduce_fusion.3
  314.2 0.7 add_convert_fusion.3
  314.9 80.0 %all-reduce.3.cloned.1.call-done = bf16[512,4096]{1,0:T(8,128)(2,1)} async-done(((bf16[512,4096]{1,0:T(8,128)(2,1)}), bf16[512,4096]{1,0:T(8,128)(2,1)}) %all-reduce.3.cloned.1.call-update) | async-done | bytes 4194320 | tf_op jit(solution)/shard_map/psum | solution.py:171
  394.9 3.1 multiply_reduce_fusion
  398.0 3.3 convert_element_type.95
  401.3 1.4 add_convert_fusion
  (65 shorter events, 2.0 us)
Async XLA Ops:
  7.2 58.1 %all-gather.9.cloned.1.call-start = ((), (), s32[]{:S(2)}) async-start(), calls=%async_computation | async-start | bytes 5242880 | tf_op jit(solution)/shard_map/all_gather | solution.py:82
  7.9 179.4 %all-gather.11.cloned.1.call-start = ((), (), s32[]{:S(2)}) async-start(), calls=%async_computation.1 | async-start | bytes 9437184 | tf_op jit(solution)/shard_map/all_gather | solution.py:130
  83.2 2.7 copy-start.1
  85.8 11.0 %copy-start.6 = (f32[1024]{0:T(1024)S(1)}, f32[1024]{0:T(1024)}, u32[]{:S(2)}) copy-start(f32[1024]{0:T(1024)} %param.15) | copy-start | bytes 12292
  85.8 12.9 %copy-start.5 = (f32[1024]{0:T(1024)S(1)}, f32[1024]{0:T(1024)}, u32[]{:S(2)}) copy-start(f32[1024]{0:T(1024)} %param.14) | copy-start | bytes 12292
  100.7 7.0 %copy-start.8 = (s32[4]{0:T(128)S(1)}, s32[4]{0:T(128)}, u32[]{:S(2)}) copy-start(s32[4]{0:T(128)} %param.17) | copy-start | bytes 52
  103.9 4.7 %copy-start = (bf16[4,128,8,128]{3,1,2,0:T(8,128)(2,1)S(1)}, bf16[4,128,8,128]{3,1,2,0:T(8,128)(2,1)}, u32[]{:S(2)}) copy-start(bf16[4,128,8,128]{3,1,2,0:T(8,128)(2,1)} %pad_maximum_fusion) | copy-start | bytes 3145732
  104.0 165.9 %all-gather.13.cloned.1.call-start = ((), (), s32[]{:S(2)}) async-start(), calls=%async_computation.2 | async-start | bytes 9437184 | tf_op jit(solution)/shard_map/all_gather | solution.py:131
  106.1 22.3 %copy-start.3 = (bf16[512,8,64]{0,2,1:T(8,128)(2,1)S(1)}, bf16[512,8,64]{0,2,1:T(8,128)(2,1)}, u32[]{:S(2)}) copy-start(bf16[512,8,64]{0,2,1:T(8,128)(2,1)} %get-tuple-element.212) | copy-start | bytes 1572868
  107.6 287.3 %all-reduce.3.cloned.1.call-start = ((), (), s32[]{:S(2)}) async-start(), calls=%async_computation.3 | async-start | bytes 8388608 | tf_op jit(solution)/shard_map/psum | solution.py:171
  291.4 22.8 %copy-start.4 = (bf16[4,1024]{1,0:T(4,128)(2,1)S(1)}, bf16[4,1024]{1,0:T(4,128)(2,1)}, u32[]{:S(2)}) copy-start(bf16[4,1024]{1,0:T(4,128)(2,1)} %param.11) | copy-start | bytes 24580
  291.4 22.8 %copy-start.7 = (f32[1024]{0:T(1024)S(1)}, f32[1024]{0:T(1024)}, u32[]{:S(2)}) copy-start(f32[1024]{0:T(1024)} %param.16) | copy-start | bytes 12292
  314.9 86.4 %copy-start.2 = (bf16[4,128,1024]{2,1,0:T(8,128)(2,1)S(1)}, bf16[4,128,1024]{2,1,0:T(8,128)(2,1)}, u32[]{:S(2)}) copy-start(bf16[4,128,1024]{2,1,0:T(8,128)(2,1)} %param.10) | copy-start | bytes 3145732
Sparse Core Ops, SparseCore 0:
  9.8 55.3 all-gather.8
  104.1 83.1 all-gather.10
  189.5 80.3 all-gather.12
  291.5 103.3 all-reduce.2
where the time goes:
time: 410 us; the launch traced here: 409 us
  waiting for transfers between devices  207 us (50%)
  blocking collectives  79.1 us (19%)
  matrix products  70.7 us (17%)
  other arithmetic  27.3 us (7%)
  between operations  14.1 us (3%)
  local copies, waits for them, and re-layouts  11.2 us (3%)
    psum x1, waiting for transfers between devices, body(): lax.psum(part_rows.astype(jnp.bfloat16), 'tp').astype(jnp.float32)  80 us
    all_gather x1, waiting for transfers between devices, body(): lax.all_gather(values, 'seq', axis=1, tiled=True)  60 us
    all_gather x3, blocking collectives, joined(): everything = jax.tree.map(lambda part: lax.all_gather(part, axis), value)  43.2 us
    all_gather x1, waiting for transfers between devices, body(): row_piece = lax.all_gather(flat_rows, 'tp', axis=1, tiled=True)  35.8 us
    all_gather x1, waiting for transfers between devices, body(): lax.all_gather(keys, 'seq', axis=1, tiled=True)  30 us
    dot_general x1, matrix products, body(): jnp.einsum('tn,cnf->ctf', row_piece, w_qkv, preferred_element_type=jnp.fl...  17.9 us
    psum x1, blocking collectives, body(): lax.psum(part_new.astype(jnp.bfloat16), 'tp').astype(jnp.float32)  17.1 us
    dot_general x1, matrix products, fold_step(): jnp.einsum('sphe,snhe->shpn', queries, key_piece, preferred_element_type=...  14 us
  transfers between devices with their start and end apart: 4, of which 4 were waited for; matrix products, arithmetic and copies ran while one was open for 12% of the time, Pallas kernels for 0%

commit v1 on v0

v1 whole, which is shorter than its diff:
```python
import jax
import jax.numpy as jnp
from jax import lax
from jax.sharding import PartitionSpec as P

HD = 128
PAD = 16
FAR = 1 << 30

rope_base = 500000.0
norm_eps = 1e-06
masked_fill = -1e30


def rope_tables(position):
    half = HD // 2
    freq = rope_base ** (-(jnp.arange(half, dtype=jnp.float32) * 2.0) / HD)
    angle = position.astype(jnp.float32)[:, None] * freq
    return jnp.cos(angle), jnp.sin(angle)


def rotate(values, cosine, sine):
    half = HD // 2
    lower = values[..., :half]
    upper = values[..., half:]
    return jnp.concatenate([lower * cosine - upper * sine, upper * cosine + lower * sine], -1)


def body(tokens, new_tokens, w_qkv, w_out, q_gain, k_gain, post_gain, lengths):
    seqs, pos_dev, width = tokens.shape
    heads = width // HD
    full = w_qkv.shape[1]
    shards = lax.axis_size("seq")
    group = shards // seqs
    piece = pos_dev // group
    me = lax.axis_index("seq")
    prompt, member = me // group, me % group
    count = shards * piece

    swapped = lax.all_to_all(tokens.reshape(shards, piece, width), "seq", 0, 0, tiled=True)
    fresh = lax.dynamic_slice_in_dim(new_tokens, prompt, 1, 0)
    rows = jnp.concatenate(
        [swapped.reshape(count, width), fresh, jnp.zeros((PAD - 1, width), tokens.dtype)], 0
    )
    everything = lax.all_gather(rows, "tp", axis=1, tiled=True)
    total = count + PAD
    proj = jnp.einsum("tn,cnf->ctf", everything, w_qkv, preferred_element_type=jnp.float32)
    squares = lax.psum(jnp.sum(proj[:2] * proj[:2], -1), "tp")
    factor = lax.rsqrt(squares / full + norm_eps)[..., None]

    length = lax.dynamic_index_in_dim(lengths, prompt, 0, keepdims=False)
    index = jnp.arange(count, dtype=jnp.int32)

    def positions(who):
        return (index // piece) * pos_dev + who * piece + index % piece

    tail = jnp.arange(PAD, dtype=jnp.int32) == 0
    position = jnp.concatenate([positions(member), jnp.where(tail, length, 0)])
    cosine, sine = rope_tables(position)
    cosine, sine = cosine[:, None], sine[:, None]

    def rotated(which, gain):
        normed = (proj[which] * factor[which] * gain).reshape(total, heads, HD)
        return rotate(normed, cosine, sine).astype(jnp.bfloat16)

    queries = rotated(0, q_gain)
    keys = rotated(1, k_gain)
    values = proj[2].astype(jnp.bfloat16).reshape(total, heads, HD)
    groups = [[b * group + g for g in range(group)] for b in range(seqs)]
    both = jnp.stack([keys[:count], values[:count]])
    gathered = lax.all_gather(both, "seq", axis=1, tiled=True, axis_index_groups=groups)
    all_keys = jnp.concatenate([gathered[0], keys[count:]], 0)
    all_values = jnp.concatenate([gathered[1], values[count:]], 0)
    key_pos = jnp.concatenate(
        [positions(g) for g in range(group)]
    )
    key_pos = jnp.concatenate([jnp.where(key_pos < length, key_pos, FAR + 1), jnp.where(tail, FAR, FAR + 1)])
    query_pos = jnp.concatenate([positions(member), jnp.where(tail, FAR, 0)])
    scores = jnp.einsum("phe,nhe->hpn", queries, all_keys, preferred_element_type=jnp.float32) * (
        HD ** (-0.5)
    )
    valid = (key_pos[None, :] <= query_pos[:, None])[None]
    scores = jnp.where(valid, scores, masked_fill)
    top = jnp.max(scores, -1, keepdims=True)
    weights = jnp.where(valid, jnp.exp(scores - top), 0.0)
    norm = jnp.sum(weights, -1)
    acc = jnp.einsum(
        "hpn,nhe->hpe", weights.astype(jnp.bfloat16), all_values, preferred_element_type=jnp.float32
    )
    attention = (acc / norm[..., None]).transpose(1, 0, 2).reshape(total, width).astype(jnp.bfloat16)

    part = jnp.dot(attention, w_out, preferred_element_type=jnp.float32).astype(jnp.bfloat16)
    own = lax.psum_scatter(part, "tp", scatter_dimension=1, tiled=True).astype(jnp.float32)
    mean = lax.psum(jnp.sum(own * own, -1), "tp") / full
    result = rows.astype(jnp.float32) + own * lax.rsqrt(mean[:, None] + norm_eps) * post_gain
    result = result.astype(jnp.bfloat16)
    out = lax.all_to_all(result[:count].reshape(shards, piece, width), "seq", 0, 0, tiled=True)
    new = lax.all_gather(result[count], "seq", axis=0)
    new = new.reshape(seqs, group, width)[:, 0]
    return out.reshape(seqs, pos_dev, width), new


def solution(mesh):
    in_specs = (
        P(None, "seq", "tp"),
        P(None, "tp"),
        P(None, None, "tp"),
        P("tp", None),
        P("tp"),
        P("tp"),
        P("tp"),
        P(),
    )
    out_specs = (P(None, "seq", "tp"), P(None, "tp"))
    return jax.shard_map(body, mesh=mesh, in_specs=in_specs, out_specs=out_specs, check_vma=False)
```

time: 410 us -> 322 us (0.79)
  waiting for transfers between devices: 207 us -> 142 us
  blocking collectives: 79.1 us -> 50.7 us
  matrix products: 70.7 us -> 55.9 us
  starting transfers between devices: 0.16 us -> 11.4 us
  other arithmetic: 27.3 us -> 33.1 us
    psum x1 -> x0, waiting for transfers between devices: 80 us -> none  [body(): lax.psum(part_rows.astype(jnp.bfloat16), 'tp').astype(jnp.float32)]
    all_gather x3 -> x2, waiting for transfers between devices: 126 us -> 60.6 us  [the longest x1 49.7 us: body(): everything = lax.all_gather(rows, 'tp', axis=1, tiled=True)]
    reduce_scatter x0 -> x1, waiting for transfers between devices: none -> 55.1 us  [body(): lax.psum_scatter(part, 'tp', scatter_dimension=1, tiled=True)]
    all_to_all x0 -> x2, waiting for transfers between devices: none -> 26.4 us  [the longest x1 26.4 us: body(): lax.all_to_all(tokens.reshape(shards, piece, width), 'seq', 0, 0, tiled=T...]
    all_gather x4 -> x1, blocking collectives: 52.9 us -> 32.7 us  [body(): new = lax.all_gather(result[count], 'seq', axis=0)]
    sub x0 -> x1, other arithmetic: none -> 18 us  [body(): weights = jnp.where(valid, jnp.exp(scores - top), 0.0)]
    dot_general x8 -> x4, matrix products: 70.7 us -> 55.9 us  [the longest x1 19.5 us: body(): jnp.einsum('tn,cnf->ctf', everything, w_qkv, preferred_element_type=jnp.f...]
    reduce_sum x5 -> x2, other arithmetic: 13.9 us -> 1.9 us  [the longest x1 1.53 us: body(): mean = lax.psum(jnp.sum(own * own, -1), 'tp') / full]
  transfers between devices with their start and end apart: 4 -> 5, of which waited for: 4 -> 4; matrix products, arithmetic and copies ran while one was open for 12% -> 2% of each run, Pallas kernels for 0% -> 0%
where the time goes in v1:
time: 322 us
  waiting for transfers between devices  142 us (44%)
  matrix products  55.9 us (17%)
  blocking collectives  50.7 us (16%)
  other arithmetic  33.1 us (10%)
  local copies, waits for them, and re-layouts  14.3 us (4%)
  between operations  14 us (4%)
  starting transfers between devices  11.4 us (4%)
    reduce_scatter x1, waiting for transfers between devices, body(): lax.psum_scatter(part, 'tp', scatter_dimension=1, tiled=True)  55.1 us
    all_gather x1, waiting for transfers between devices, body(): everything = lax.all_gather(rows, 'tp', axis=1, tiled=True)  49.7 us
    all_gather x1, blocking collectives, body(): new = lax.all_gather(result[count], 'seq', axis=0)  32.7 us
    all_to_all x1, waiting for transfers between devices, body(): lax.all_to_all(tokens.reshape(shards, piece, width), 'seq', 0, 0, tiled=T...  26.4 us
    dot_general x1, matrix products, body(): jnp.einsum('tn,cnf->ctf', everything, w_qkv, preferred_element_type=jnp.f...  19.5 us
    sub x1, other arithmetic, body(): weights = jnp.where(valid, jnp.exp(scores - top), 0.0)  18 us
    dot_general x1, matrix products, body(): jnp.einsum('hpn,nhe->hpe', weights.astype(jnp.bfloat16), all_values, pref...  17.4 us
    all_gather x1, waiting for transfers between devices, body(): lax.all_gather(both, 'seq', axis=1, tiled=True, axis_index_groups=groups)  10.9 us
  transfers between devices with their start and end apart: 5, of which 4 were waited for; matrix products, arithmetic and copies ran while one was open for 2% of the time, Pallas kernels for 0%

profile of v1, /device:TPU:0, one launch (start us, length us, event | category | flops | bytes accessed | tf_op | source)
XLA Modules:
  0.0 321.5 jit_solution(5897545532661606569)
XLA Ops:
  7.2 0.0 copy-start
  7.2 6.3 %all-to-all-start = ((bf16[8,64,1024]{2,1,0:T(8,128)(2,1)}), bf16[8,64,1024]{2,1,0:T(8,128)(2,1)S(1)}, u32[]{:S(2)}, u32[]{:S(2)}) async-start(bf16[8,64,1024]{2,1,0:T(8,128)(2,1)} %bitcast.66), calls=%async_computation | async-start | bytes 2097152 | tf_op jit(solution)/shard_map/all_to_all | solution.py:40
  13.5 0.0 all-gather.4.cloned.1.call-start
  13.6 0.1 pad.20.clone
  13.7 26.4 %all-to-all-done = bf16[8,64,1024]{2,1,0:T(8,128)(2,1)S(1)} async-done(((bf16[8,64,1024]{2,1,0:T(8,128)(2,1)}), bf16[8,64,1024]{2,1,0:T(8,128)(2,1)S(1)}, u32[]{:S(2)}, u32[]{:S(2)}) %all-to-all-start) | async-done | bytes 1048608 | tf_op jit(solution)/shard_map/all_to_all | solution.py:40
  40.1 1.2 maximum_maximum_fusion
  41.3 0.0 all-gather.4.cloned.1.call-update
  41.4 0.0 all-gather.6.cloned.1.call-start
  41.4 0.6 dynamic_slice.8
  42.0 0.7 fusion.58
  42.7 1.8 multiply_cosine_fusion
  44.5 49.7 %all-gather.4.cloned.1.call-done = bf16[528,4096]{1,0:T(8,128)(2,1)} async-done(((bf16[528,1024]{1,0:T(8,128)(2,1)}), bf16[528,4096]{1,0:T(8,128)(2,1)}) %all-gather.4.cloned.1.call-update) | async-done | bytes 4325392 | tf_op jit(solution)/shard_map/all_gather | solution.py:45
  94.2 19.5 %fusion.65 = (bf16[3,528,1024]{2,1,0:T(8,128)(2,1)}, f32[3,528,1024]{2,1,0:T(8,128)S(1)}) fusion(bf16[3,4096,1024]{2,1,0:T(8,128)(2,1)} %param.10, bf16[528,4096]{1,0:T(8,128)(2,1)} %all-gather.4.cloned.1.call-done), kind=kOutput, calls=%fused_computation.103 | convolution fusion | flops 13289177088 | bytes 39223296 | tf_op jit(solution)/shard_map/tn,cnf->ctf/dot_general | solution.py:47
  113.8 0.4 fusion.8
  114.1 2.0 slice_bitcast_fusion.1
  116.1 0.5 copy.33
  116.6 9.1 %psum.14 = f32[2,528]{1,0:T(2,128)S(1)} all-reduce(f32[2,528]{1,0:T(2,128)S(1)} %fusion.8), channel_id=1, replica_groups=mesh['seq'=8,'tp'=4] {'tp'}, use_global_device_ids=true, to_apply=%region_1.2 | all-reduce | flops 1056 | bytes 8448 | tf_op jit(solution)/shard_map/psum | solution.py:48
  125.7 1.4 copy_bitcast_fusion
  127.1 0.0 copy-start.7
  127.2 0.0 copy-start.8
  127.2 2.1 copy.34
  129.3 0.9 fusion.21
  130.2 0.1 copy-done.5
  130.2 2.7 subtract_convert_fusion.1
  133.0 0.6 fusion.42
  133.6 1.6 pad_maximum_fusion
  135.1 0.0 all-gather.6.cloned.1.call-update
  135.2 0.2 reduce-scatter.2.cloned.1.call-start
  135.4 0.7 compare_select_fusion
  136.1 1.2 broadcast_compare_fusion
  137.3 0.8 slice_bitcast_fusion.5
  138.1 10.9 %all-gather.6.cloned.1.call-done = bf16[2,1024,8,128]{3,1,2,0:T(8,128)(2,1)} async-done(((bf16[2,512,8,128]{3,1,2,0:T(8,128)(2,1)}), bf16[2,1024,8,128]{3,1,2,0:T(8,128)(2,1)}) %all-gather.6.cloned.1.call-update) | async-done | bytes 4194320 | tf_op jit(solution)/shard_map/all_gather | solution.py:71
  149.0 4.0 %slice_bitcast_fusion.2 = (bf16[1024,8,128]{2,0,1:T(8,128)(2,1)}, bf16[1024,8,128]{2,0,1:T(8,128)(2,1)S(1)}) fusion(bf16[2,1024,8,128]{3,1,2,0:T(8,128)(2,1)} %all-gather.6.cloned.1.call-done), kind=kLoop, calls=%fused_computation.45 | loop fusion | bytes 8388608 | tf_op jit(solution)/shard_map/squeeze | solution.py:73
  153.0 8.7 %multiply_select_fusion = f32[8,528,1040]{2,1,0:T(8,128)} fusion(pred[528,1040]{1,0:T(8,128)(4,1)S(1)} %copy-done.6, bf16[528,8,64]{2,0,1:T(8,128)(2,1)S(1)} %get-tuple-element.12, bf16[528,8,64]{2,0,1:T(8,128)(2,1)S(1)} %get-tuple-element.13, bf16[1024,8,128]{2,0,1:T(8,128)(2,1)S(1)} %get-tuple-element.7, bf16[528,8,64]{2,0,1:T(8,128)(2,1)S(1)} %copy-done.4, ...), kind=kOutput, calls=%fused_computation.3 | convolution fusion | flops 1145131008 | bytes 22380800 | tf_op jit(solution)/shard_map/phe,nhe->hpn/dot_general | solution.py:79
  161.7 18.0 %fusion.2 = f32[8,528]{1,0:T(8,128)S(1)} fusion(pred[528,1040]{1,0:T(8,128)(4,1)} %broadcast_compare_fusion, f32[8,528,1040]{2,1,0:T(8,128)} %multiply_select_fusion), kind=kOutput, calls=%fused_computation.4 | output fusion | flops 13179919 | bytes 18137856 | tf_op jit(solution)/shard_map/sub | solution.py:85
  179.7 17.4 %fusion.39 = bf16[8,66,8,128]{3,2,1,0:T(8,128)(2,1)} fusion(f32[528,8]{0,1:T(8,128)S(1)} %bitcast.72, bf16[16,8,128]{2,0,1:T(8,128)(2,1)S(1)} %copy.27, bf16[1024,8,128]{2,0,1:T(8,128)(2,1)S(1)} %copy-done.2, pred[528,1040]{1,0:T(8,128)(4,1)} %broadcast_compare_fusion, f32[8,528,1040]{2,1,0:T(8,128)} %multiply_select_fusion), kind=kOutput, calls=%fused_computation.57 | convolution fusion | flops 1143123072 | bytes 21349120 | tf_op jit(solution)/shard_map/hpn,nhe->hpe/dot_general | solution.py:87
  197.1 10.4 %convolution_convert_fusion = bf16[528,4096]{1,0:T(8,128)(2,1)} fusion(bf16[1024,4096]{1,0:T(8,128)(2,1)} %param.11, bf16[8,66,8,128]{3,2,1,0:T(8,128)(2,1)} %fusion.39), kind=kOutput, calls=%fused_computation.9 | convolution fusion | flops 4431347712 | bytes 13795328 | tf_op jit(solution)/shard_map/dot_general | solution.py:92
  207.5 0.0 reduce-scatter.2.cloned.1.call-update
  207.5 55.1 %reduce-scatter.2.cloned.1.call-done = bf16[528,1024]{1,0:T(8,128)(2,1)} async-done(((bf16[528,4096]{1,0:T(8,128)(2,1)}), bf16[528,1024]{1,0:T(8,128)(2,1)}) %reduce-scatter.2.cloned.1.call-update) | async-done | bytes 1081360 | tf_op jit(solution)/shard_map/reduce_scatter | solution.py:93
  262.6 1.5 fusion.16
  264.1 8.9 %psum.15 = f32[528]{0:T(1024)S(1)} all-reduce(f32[528]{0:T(1024)S(1)} %fusion.16), channel_id=1, replica_groups=mesh['seq'=8,'tp'=4] {'tp'}, use_global_device_ids=true, to_apply=%region_6.7 | all-reduce | flops 528 | bytes 4224 | tf_op jit(solution)/shard_map/psum | solution.py:94
  273.0 1.8 fusion.19
  274.8 1.0 slice.101
  275.9 4.8 %all-to-all-start.1 = ((bf16[8,64,1024]{2,1,0:T(8,128)(2,1)}), bf16[8,64,1024]{2,1,0:T(8,128)(2,1)S(1)}, u32[]{:S(2)}, u32[]{:S(2)}) async-start(bf16[8,64,1024]{2,1,0:T(8,128)(2,1)} %bitcast.12), calls=%async_computation.2 | async-start | bytes 2097152 | tf_op jit(solution)/shard_map/all_to_all | solution.py:97
  280.6 32.7 %all-gather = bf16[8,1,1024]{2,1,0:T(2,128)(2,1)S(1)} all-gather(bf16[1,1,1024]{2,1,0:T(2,128)(2,1)S(1)} %slice_bitcast_fusion.6), channel_id=1, replica_groups=mesh['seq'=8,'tp'=4] {'seq'}, dimensions={0}, use_global_device_ids=true | all-gather | bytes 18432 | tf_op jit(solution)/shard_map/all_gather | solution.py:98
  313.3 0.1 reduce.2
  313.4 0.6 copy.48
  314.0 1.0 copy.50
  (34 shorter events, 0.2 us)
Async XLA Ops:
  7.2 6.5 %copy-start = (bf16[4,1024]{1,0:T(4,128)(2,1)S(1)}, bf16[4,1024]{1,0:T(4,128)(2,1)}, u32[]{:S(2)}) copy-start(bf16[4,1024]{1,0:T(4,128)(2,1)} %param.9) | copy-start | bytes 24580
  7.2 32.9 %all-to-all-start = ((bf16[8,64,1024]{2,1,0:T(8,128)(2,1)}), bf16[8,64,1024]{2,1,0:T(8,128)(2,1)S(1)}, u32[]{:S(2)}, u32[]{:S(2)}) async-start(bf16[8,64,1024]{2,1,0:T(8,128)(2,1)} %bitcast.66), calls=%async_computation | async-start | bytes 2097152 | tf_op jit(solution)/shard_map/all_to_all | solution.py:40
  13.5 27.9 %copy-start.10 = (s32[4]{0:T(128)S(1)}, s32[4]{0:T(128)}, u32[]{:S(2)}) copy-start(s32[4]{0:T(128)} %param.15) | copy-start | bytes 52
  13.5 80.7 %all-gather.4.cloned.1.call-start = ((), (), s32[]{:S(2)}) async-start(), calls=%async_computation.3 | async-start | bytes 5406720 | tf_op jit(solution)/shard_map/all_gather | solution.py:45
  41.4 107.6 %all-gather.6.cloned.1.call-start = ((), (), s32[]{:S(2)}) async-start(), calls=%async_computation.4 | async-start | bytes 6291456 | tf_op jit(solution)/shard_map/all_gather | solution.py:71
  127.1 2.1 copy-start.7
  127.2 2.1 copy-start.8
  129.3 1.0 copy-start.5
  135.2 127.4 %reduce-scatter.2.cloned.1.call-start = ((), (), s32[]{:S(2)}) async-start(), calls=%async_computation.5 | async-start | bytes 5406720 | tf_op jit(solution)/shard_map/reduce_scatter | solution.py:93
  149.0 4.0 %copy-start.3 = (bf16[528,8,64]{2,0,1:T(8,128)(2,1)S(1)}, bf16[528,8,64]{2,0,1:T(8,128)(2,1)}, u32[]{:S(2)}) copy-start(bf16[528,8,64]{2,0,1:T(8,128)(2,1)} %get-tuple-element.8) | copy-start | bytes 1622020
  149.0 4.0 %copy-start.4 = (bf16[528,8,64]{2,0,1:T(8,128)(2,1)S(1)}, bf16[528,8,64]{2,0,1:T(8,128)(2,1)}, u32[]{:S(2)}) copy-start(bf16[528,8,64]{2,0,1:T(8,128)(2,1)} %get-tuple-element.9) | copy-start | bytes 1622020
  149.0 4.0 %copy-start.6 = (pred[528,1040]{1,0:T(8,128)(4,1)S(1)}, pred[528,1040]{1,0:T(8,128)(4,1)}, u32[]{:S(2)}) copy-start(pred[528,1040]{1,0:T(8,128)(4,1)} %broadcast_compare_fusion) | copy-start | bytes 1647364
  161.7 18.0 %copy-start.2 = (bf16[1024,8,128]{2,0,1:T(8,128)(2,1)S(1)}, bf16[1024,8,128]{2,0,1:T(8,128)(2,1)}, u32[]{:S(2)}) copy-start(bf16[1024,8,128]{2,0,1:T(8,128)(2,1)} %get-tuple-element.6) | copy-start | bytes 6291460
  207.5 65.6 %copy-start.9 = (f32[1024]{0:T(1024)S(1)}, f32[1024]{0:T(1024)}, u32[]{:S(2)}) copy-start(f32[1024]{0:T(1024)} %param.14) | copy-start | bytes 12292
  275.9 39.1 %copy-start.1 = (bf16[4,1024]{1,0:T(4,128)(2,1)S(1)}, bf16[4,1024]{1,0:T(4,128)(2,1)}, u32[]{:S(2)}) copy-start(bf16[4,1024]{1,0:T(4,128)(2,1)} %param.9) | copy-start | bytes 24580
  275.9 38.2 %all-to-all-start.1 = ((bf16[8,64,1024]{2,1,0:T(8,128)(2,1)}), bf16[8,64,1024]{2,1,0:T(8,128)(2,1)S(1)}, u32[]{:S(2)}, u32[]{:S(2)}) async-start(bf16[8,64,1024]{2,1,0:T(8,128)(2,1)} %bitcast.12), calls=%async_computation.2 | async-start | bytes 2097152 | tf_op jit(solution)/shard_map/all_to_all | solution.py:97
Sparse Core Ops, SparseCore 0:
  41.5 52.6 all-gather.3
  135.3 13.6 all-gather.5
  207.6 54.9 reduce-scatter.1

commit v2 on v1

--- a/solution.py
+++ b/solution.py
@@ -1,6 +1,10 @@
+from functools import partial
+
 import jax
 import jax.numpy as jnp
 from jax import lax
+from jax.experimental import pallas as pl
+from jax.experimental.pallas import tpu as pltpu
 from jax.sharding import PartitionSpec as P
 
 HD = 128
@@ -100,6 +104,343 @@
     return out.reshape(seqs, pos_dev, width), new
 
 
+MESH = pl.DeviceIdType.MESH
+VMEM_LIMIT = 60 << 20
+ROWS = 128
+
+
+def remote(src, dst, send, recv, target):
+    return pltpu.make_async_remote_copy(
+        src_ref=src, dst_ref=dst, send_sem=send, recv_sem=recv, device_id=target, device_id_type=MESH
+    )
+
+
+def greet(targets):
+    barrier = pltpu.get_barrier_semaphore()
+    for target in targets:
+        pl.semaphore_signal(barrier, inc=1, device_id=target, device_id_type=MESH)
+    pl.semaphore_wait(barrier, len(targets))
+
+
+def gather_project(shards, piece, tok, new, w, rows, raw, value, x, wv, acc, w_sem, loc_sem, a_send, a_recv, g_send, g_recv, n_send, n_recv):
+    me, t = lax.axis_index("seq"), lax.axis_index("tp")
+    width = tok.shape[2]
+    count = shards * piece
+    half = piece // 2
+    near = [{"tp": t ^ j} for j in range(1, 4)]
+    loads = []
+    for j in range(4):
+        load = pltpu.make_async_copy(w.at[:, pl.ds((t ^ j) * width, width), :], wv.at[j], w_sem.at[j])
+        load.start()
+        loads.append(load)
+    own = pltpu.make_async_copy(tok.at[me], x.at[0, pl.ds(0, piece)], loc_sem.at[0])
+    own.start()
+    fresh = pltpu.make_async_copy(new, x.at[0, pl.ds(count, PAD)], loc_sem.at[1])
+    fresh.start()
+    greet([{"seq": me ^ k} for k in range(1, shards)] + near)
+
+    swaps = []
+    for k in range(1, shards):
+        copy = remote(tok.at[me ^ k], x.at[0, pl.ds(k * piece, piece)], a_send.at[k], a_recv.at[k], {"seq": me ^ k})
+        copy.start()
+        swaps.append(copy)
+
+    def first(j, k):
+        at = x.at[0, pl.ds(k * piece, piece)]
+        return remote(at, x.at[j, pl.ds(k * piece, piece)], g_send.at[j - 1, k], g_recv.at[j - 1, k], near[j - 1])
+
+    def second(j, k):
+        start = k * piece + (j - 1) * half
+        return remote(
+            x.at[j, pl.ds(start, half)], x.at[3, pl.ds(start, half)],
+            g_send.at[1 + j, k], g_recv.at[1 + j, k], near[2 - j],
+        )
+
+    def tail(j):
+        at = x.at[0, pl.ds(count, PAD)]
+        return remote(at, x.at[j, pl.ds(count, PAD)], n_send.at[j - 1], n_recv.at[j - 1], near[j - 1])
+
+    def multiply(j, start, size, clear):
+        def tile(i, carry):
+            c, col = i // 2, pl.ds(pl.multiple_of((i % 2) * (width // 2), width // 2), width // 2)
+            part = jnp.dot(x[j, pl.ds(start, size), :], wv[j, c, :, col], preferred_element_type=jnp.float32)
+            if clear:
+                acc[c, pl.ds(start, size), col] = part
+            else:
+                acc[c, pl.ds(start, size), col] += part
+            return carry
+
+        lax.fori_loop(0, 6, tile, 0)
+
+    def arrive(k):
+        if k == 0:
+            own.wait()
+        else:
+            swaps[k - 1].wait_recv()
+        first(1, k).start()
+        first(2, k).start()
+
+    def forward(k):
+        first(1, k).wait_recv()
+        second(1, k).start()
+        first(2, k).wait_recv()
+        second(2, k).start()
+
+    middle = shards // 2
+    low, high = middle * piece, count - middle * piece + PAD
+    for k in range(shards):
+        arrive(k)
+        if k == 0:
+            fresh.wait()
+            for j in range(1, 4):
+                tail(j).start()
+        if k >= 1:
+            forward(k - 1)
+        if k == middle:
+            loads[0].wait()
+            multiply(0, 0, low, True)
+        if k == middle + 1:
+            loads[1].wait()
+            multiply(1, 0, low, False)
+        if k == middle + 2:
+            loads[2].wait()
+            multiply(2, 0, low, False)
+    forward(shards - 1)
+    multiply(0, low, high, True)
+    loads[3].wait()
+    for k in range(middle):
+        second(1, k).wait_recv()
+        second(2, k).wait_recv()
+    multiply(3, 0, low, False)
+    for j in range(1, 4):
+        tail(j).wait_recv()
+    multiply(1, low, high, False)
+    multiply(2, low, high, False)
+    for k in range(middle, shards):
+        second(1, k).wait_recv()
+        second(2, k).wait_recv()
+    multiply(3, low, high, False)
+    raw[...] = acc[0:2]
+    value[...] = acc[2].astype(jnp.bfloat16)
+    rows[...] = x[0]
+    for copy in swaps:
+        copy.wait_send()
+    for k in range(shards):
+        for j in (1, 2):
+            first(j, k).wait_send()
+            second(j, k).wait_send()
+    for j in range(1, 4):
+        tail(j).wait_send()
+
+
+def flat_tile(column):
+    size = column.shape[0]
+    wide = jnp.broadcast_to(column, (size, ROWS))
+    if size < ROWS:
+        wide = jnp.concatenate([wide, jnp.zeros((ROWS - size, ROWS), jnp.float32)], 0)
+    return wide.T[0:8]
+
+
+def tall_tile(flat, size):
+    return jnp.broadcast_to(flat[0:1], (ROWS, ROWS)).T[0:size]
+
+
+def lanes(block):
+    total = block[:, 0:HD]
+    for h in range(1, block.shape[1] // HD):
+        total = total + block[:, h * HD : (h + 1) * HD]
+    return total
+
+
+def attend(full, raw, value, cos, sin, qpos, kpos, qg, kg, out, sq, sq_in, q, ka, va, bias, s_send, s_recv, p_send, p_recv, loc_sem):
+    me, t = lax.axis_index("seq"), lax.axis_index("tp")
+    total, width = value.shape
+    count = total - PAD
+    heads = width // HD
+    near = [{"tp": t ^ j} for j in range(1, 4)]
+    mate = {"seq": me ^ 1}
+    spans = [(i * ROWS, ROWS) for i in range(count // ROWS)] + [(count, PAD)]
+    tiles = len(spans)
+    greet(near + [mate])
+    send_v = remote(value.at[pl.ds(0, count)], va.at[pl.ds(count, count)], p_send.at[0], p_recv.at[0], mate)
+    send_v.start()
+    for which in range(2):
+        for i, (start, size) in enumerate(spans):
+            block = raw[which, start : start + size, :]
+            column = jnp.sum(lanes(block * block), -1, keepdims=True)
+            sq[which * tiles + i] = flat_tile(column)
+    squares = [remote(sq, sq_in.at[j], s_send.at[j], s_recv.at[j], near[j]) for j in range(3)]
+    for copy in squares:
+        copy.start()
+    va[0:count, :] = value[0:count, :]
+    va[2 * count :, :] = value[count:, :]
+    for start, size in spans:
+        bias[start : start + size, :] = jnp.where(kpos[...] <= qpos[start : start + size, :], 0.0, masked_fill)
+    for copy in squares:
+        copy.wait_recv()
+
+    def finish(which, gain, start, size, i):
+        slot = which * tiles + i
+        flat = sq[slot] + sq_in[0, slot] + sq_in[1, slot] + sq_in[2, slot]
+        factor = lax.rsqrt(tall_tile(flat, size) / full + norm_eps)
+        c, s = cos[start : start + size, :], sin[start : start + size, :]
+        parts = []
+        for h in range(heads):
+            at = slice(h * HD, (h + 1) * HD)
+            normed = raw[which, start : start + size, at] * factor * gain[:, at]
+            parts.append((normed * c + pltpu.roll(normed, HD // 2, 1) * s).astype(jnp.bfloat16))
+        return jnp.concatenate(parts, -1)
+
+    for i, (start, size) in enumerate(spans):
+        place = start if start < count else 2 * count
+        ka[place : place + size, :] = finish(1, kg, start, size, i)
+    send_k = remote(ka.at[pl.ds(0, count)], ka.at[pl.ds(count, count)], p_send.at[1], p_recv.at[1], mate)
+    send_k.start()
+    for i, (start, size) in enumerate(spans):
+        q[start : start + size, :] = finish(0, qg, start, size, i)
+    send_v.wait_recv()
+    send_k.wait_recv()
+
+    def one_head(h, carry):
+        at = pl.ds(pl.multiple_of(h * HD, HD), HD)
+        for start, size in spans:
+            scores = lax.dot_general(
+                q[start : start + size, at], ka[:, at], (((1,), (1,)), ((), ())), preferred_element_type=jnp.float32
+            )
+            scores = scores + bias[start : start + size, :]
+            top = jnp.max(scores, -1, keepdims=True)
+            weights = jnp.exp((scores - top) * (HD ** (-0.5)))
+            norm = jnp.sum(weights, -1, keepdims=True)
+            mixed = jnp.dot(weights.astype(jnp.bfloat16), va[:, at], preferred_element_type=jnp.float32)
+            out[start : start + size, at] = (mixed / norm).astype(jnp.bfloat16)
+        return carry
+
+    lax.fori_loop(0, heads, one_head, 0)
+    for copy in squares:
+        copy.wait_send()
+    send_v.wait_send()
+    send_k.wait_send()
+
+
+def in_vmem():
+    return pl.BlockSpec(memory_space=pltpu.VMEM)
+
+
+def call_gather(tokens, new, w_qkv, shards, piece):
+    width = tokens.shape[2]
+    total = shards * piece + PAD
+    dma = pltpu.SemaphoreType.DMA
+    return pl.pallas_call(
+        partial(gather_project, shards, piece),
+        out_shape=(
+            jax.ShapeDtypeStruct((total, width), jnp.bfloat16),
+            jax.ShapeDtypeStruct((2, total, width), jnp.float32),
+            jax.ShapeDtypeStruct((total, width), jnp.bfloat16),
+        ),
+        in_specs=[in_vmem(), in_vmem(), pl.BlockSpec(memory_space=pl.ANY)],
+        out_specs=(in_vmem(), in_vmem(), in_vmem()),
+        scratch_shapes=[
+            pltpu.VMEM((4, total, width), jnp.bfloat16),
+            pltpu.VMEM((4, 3, width, width), jnp.bfloat16),
+            pltpu.VMEM((3, total, width), jnp.float32),
+            dma((4,)),
+            dma((2,)),
+            dma((shards,)),
+            dma((shards,)),
+            dma((4, shards)),
+            dma((4, shards)),
+            dma((3,)),
+            dma((3,)),
+        ],
+        compiler_params=pltpu.CompilerParams(collective_id=0, has_side_effects=True, vmem_limit_bytes=VMEM_LIMIT),
+        name="gather_project",
+    )(tokens, new, w_qkv)
+
+
+def call_attend(full, raw, value, cos, sin, qpos, kpos, qg, kg):
+    total, width = value.shape
+    keys = 2 * (total - PAD) + PAD
+    tiles = (total - PAD) // ROWS + 1
+    dma = pltpu.SemaphoreType.DMA
+    return pl.pallas_call(
+        partial(attend, full),
+        out_shape=jax.ShapeDtypeStruct((total, width), jnp.bfloat16),
+        in_specs=[in_vmem()] * 8,
+        out_specs=in_vmem(),
+        scratch_shapes=[
+            pltpu.VMEM((2 * tiles, 8, ROWS), jnp.float32),
+            pltpu.VMEM((3, 2 * tiles, 8, ROWS), jnp.float32),
+            pltpu.VMEM((total, width), jnp.bfloat16),
+            pltpu.VMEM((keys, width), jnp.bfloat16),
+            pltpu.VMEM((keys, width), jnp.bfloat16),
+            pltpu.VMEM((total, keys), jnp.float32),
+            dma((3,)),
+            dma((3,)),
+            dma((2,)),
+            dma((2,)),
+            dma((1,)),
+        ],
+        compiler_params=pltpu.CompilerParams(collective_id=1, has_side_effects=True, vmem_limit_bytes=VMEM_LIMIT),
+        name="attend",
+    )(raw, value, cos, sin, qpos, kpos, qg, kg)
+
+
+def fast_body(tokens, new_tokens, w_qkv, w_out, q_gain, k_gain, post_gain, lengths):
+    seqs, pos_dev, width = tokens.shape
+    full = w_qkv.shape[1]
+    shards = lax.axis_size("seq")
+    group = shards // seqs
+    piece = pos_dev // group
+    me = lax.axis_index("seq")
+    prompt, member = me // group, me % group
+    count = shards * piece
+    fresh = lax.dynamic_slice_in_dim(new_tokens, prompt, 1, 0)
+    fresh = jnp.pad(fresh, ((0, PAD - 1), (0, 0)))
+    rows, raw, value = call_gather(tokens.reshape(shards, piece, width), fresh, w_qkv, shards, piece)
+
+    length = lax.dynamic_index_in_dim(lengths, prompt, 0, keepdims=False)
+    index = jnp.arange(count, dtype=jnp.int32)
+
+    def positions(who):
+        return ((index // piece) ^ who) * pos_dev + (who % group) * piece + index % piece
+
+    tail = jnp.arange(PAD, dtype=jnp.int32) == 0
+    position = jnp.concatenate([positions(me), jnp.where(tail, length, 0)])
+    cosine, sine = rope_tables(position)
+    cos = jnp.concatenate([cosine, cosine], -1)
+    sin = jnp.concatenate([-sine, sine], -1)
+    key_pos = jnp.concatenate([positions(me), positions(me ^ 1)])
+    key_pos = jnp.concatenate(
+        [jnp.where(key_pos < length, key_pos, FAR + 1), jnp.where(tail, FAR, FAR + 1)]
+    )
+    query_pos = jnp.concatenate([positions(me), jnp.where(tail, FAR, 0)])
+    attention = call_attend(
+        full, raw, value, cos, sin, query_pos[:, None], key_pos[None, :], q_gain[None], k_gain[None]
+    )
+    return finish_fast(attention, w_out, rows, post_gain, full, seqs, pos_dev)
+
+
+def finish_fast(attention, w_out, rows, post_gain, full, seqs, pos_dev):
+    width = rows.shape[1]
+    shards = lax.axis_size("seq")
+    group = shards // seqs
+    piece = pos_dev // group
+    me = lax.axis_index("seq")
+    count = shards * piece
+    part = jnp.dot(attention, w_out, preferred_element_type=jnp.float32).astype(jnp.bfloat16)
+    own = lax.psum_scatter(part, "tp", scatter_dimension=1, tiled=True).astype(jnp.float32)
+    mean = lax.psum(jnp.sum(own * own, -1), "tp") / full
+    result = rows.astype(jnp.float32) + own * lax.rsqrt(mean[:, None] + norm_eps) * post_gain
+    result = result.astype(jnp.bfloat16)
+    blocks = jnp.stack(
+        [lax.dynamic_slice_in_dim(result, (me ^ k) * piece, piece, 0) for k in range(shards)]
+    )
+    out = lax.all_to_all(blocks, "seq", 0, 0, tiled=True)
+    new = lax.all_gather(result[count], "seq", axis=0)
+    new = new.reshape(seqs, group, width)[:, 0]
+    return out.reshape(seqs, pos_dev, width), new
+
+
 def solution(mesh):
     in_specs = (
         P(None, "seq", "tp"),
@@ -112,4 +453,5 @@
         P(),
     )
     out_specs = (P(None, "seq", "tp"), P(None, "tp"))
-    return jax.shard_map(body, mesh=mesh, in_specs=in_specs, out_specs=out_specs, check_vma=False)
+    chosen = fast_body if (mesh.shape["seq"], mesh.shape["tp"]) == (8, 4) else body
+    return jax.shard_map(chosen, mesh=mesh, in_specs=in_specs, out_specs=out_specs, check_vma=False)

time: 322 us -> 232 us (0.72)
  Pallas kernels: 0 us -> 89.9 us
  waiting for transfers between devices: 142 us -> 53.4 us
  matrix products: 55.9 us -> 10.4 us
  other arithmetic: 33.1 us -> 6.24 us
  blocking collectives: 50.7 us -> 41.6 us
  starting transfers between devices: 11.4 us -> 4.62 us
  local copies, waits for them, and re-layouts: 14.3 us -> 10.8 us
    pallas_call x0 -> x2, Pallas kernels: none -> 89.9 us  [the longest x1 61.2 us: call_gather(): pl.pallas_call(partial(gather_project, shards, piece), out_shape=(jax.Sha...]
    all_gather x2 -> x0, waiting for transfers between devices: 60.6 us -> none  [the longest x1 49.7 us: body(): everything = lax.all_gather(rows, 'tp', axis=1, tiled=True)]
    dot_general x4 -> x1, matrix products: 55.9 us -> 10.4 us  [finish_fast(): jnp.dot(attention, w_out, preferred_element_type=jnp.float32)]
    all_to_all x2 -> x1, waiting for transfers between devices: 26.4 us -> 0.01 us  [finish_fast(): out = lax.all_to_all(blocks, 'seq', 0, 0, tiled=True)]
    sub x1 -> x0, other arithmetic: 18 us -> none  [body(): weights = jnp.where(valid, jnp.exp(scores - top), 0.0)]
    psum x2 -> x1, blocking collectives: 18 us -> 8.93 us  [finish_fast(): mean = lax.psum(jnp.sum(own * own, -1), 'tp') / full]
    all_to_all x2 -> x1, starting transfers between devices: 11.1 us -> 4.58 us  [finish_fast(): out = lax.all_to_all(blocks, 'seq', 0, 0, tiled=True)]
    another operation x3 -> x0, other arithmetic: 4.88 us -> none
  transfers between devices with their start and end apart: 5 -> 2, of which waited for: 4 -> 1; matrix products, arithmetic and copies ran while one was open for 2% -> 0% of each run, Pallas kernels for 0% -> 0%
where the time goes in v2:
time: 232 us; the launch traced here: 231 us
  Pallas kernels  89.9 us (39%)
  waiting for transfers between devices  53.4 us (23%)
  blocking collectives  41.6 us (18%)
  between operations  14.3 us (6%)
  local copies, waits for them, and re-layouts  10.8 us (5%)
  matrix products  10.4 us (4%)
  other arithmetic  6.24 us (3%)
  starting transfers between devices  4.62 us (2%)
    pallas_call x1, Pallas kernels, call_gather(): pl.pallas_call(partial(gather_project, shards, piece), out_shape=(jax.Sha...  61.2 us
    reduce_scatter x1, waiting for transfers between devices, finish_fast(): lax.psum_scatter(part, 'tp', scatter_dimension=1, tiled=True)  53.4 us
    all_gather x1, blocking collectives, finish_fast(): new = lax.all_gather(result[count], 'seq', axis=0)  32.7 us
    pallas_call x1, Pallas kernels, call_attend(): pl.pallas_call(partial(attend, full), out_shape=jax.ShapeDtypeStruct((tot...  28.7 us
    dot_general x1, matrix products, finish_fast(): jnp.dot(attention, w_out, preferred_element_type=jnp.float32)  10.4 us
    psum x1, blocking collectives, finish_fast(): mean = lax.psum(jnp.sum(own * own, -1), 'tp') / full  8.93 us
    unnamed x18, local copies, waits for them, and re-layouts  6.81 us
  transfers between devices with their start and end apart: 2, of which 1 were waited for; matrix products, arithmetic and copies ran while one was open for 0% of the time, Pallas kernels for 0%

profile of v2, /device:TPU:0, one launch (start us, length us, event | category | flops | bytes accessed | tf_op | source)
XLA Modules:
  0.0 231.2 jit_solution(2129499357521941501)
XLA Ops:
  7.2 0.0 copy-start
  7.2 0.0 reduce-scatter.2.cloned.1.call-start
  7.3 0.6 copy-done
  7.9 1.2 dynamic_slice.32
  9.1 0.6 fusion.23
  9.8 1.0 fusion.4
  10.8 0.8 pad_maximum_fusion.cos
  11.7 0.8 broadcast_in_dim.44.qpos
  12.5 0.7 compare_select_fusion
  13.2 0.6 broadcast_in_dim.41.kpos
  13.8 0.6 pad.4.new
  14.4 0.9 pad_maximum_fusion.1.sin
  15.3 61.2 %gather_project.1 = (bf16[528,1024]{1,0:T(8,128)(2,1)}, f32[2,528,1024]{2,1,0:T(8,128)}, bf16[528,1024]{1,0:T(8,128)(2,1)}) custom-call(bf16[8,64,1024]{2,1,0:T(8,128)(2,1)} %bitcast.30, bf16[16,1024]{1,0:T(8,128)(2,1)} %pad.4.new, bf16[3,4096,1024]{2,1,0:T(8,128)(2,1)} %w.1), custom_call_target="tpu_custom_call" | custom-call | tf_op jit(solution)/shard_map/gather_project/pallas_call | solution.py:333
  76.5 28.7 %attend.1 = bf16[528,1024]{1,0:T(8,128)(2,1)} custom-call(f32[2,528,1024]{2,1,0:T(8,128)} %get-tuple-element.6.raw, bf16[528,1024]{1,0:T(8,128)(2,1)} %get-tuple-element.7.value, f32[528,128]{1,0:T(8,128)} %pad_maximum_fusion.cos, f32[528,128]{1,0:T(8,128)} %pad_maximum_fusion.1.sin, s32[528,1]{1,0:T(8,128)} %broadcast_in_dim.44.qpos, ...), custom_call_target="tpu_custom_call" | custom-call | tf_op jit(solution)/shard_map/attend/pallas_call | solution.py:365
  105.2 10.4 %convolution_convert_fusion = bf16[528,4096]{1,0:T(8,128)(2,1)} fusion(bf16[528,1024]{1,0:T(8,128)(2,1)} %attend.1, bf16[1024,4096]{1,0:T(8,128)(2,1)} %param.11), kind=kOutput, calls=%fused_computation | convolution fusion | flops 4431347712 | bytes 13795328 | tf_op jit(solution)/shard_map/dot_general | solution.py:430
  115.6 0.0 copy-start.2
  115.6 0.0 reduce-scatter.2.cloned.1.call-update
  115.6 0.0 copy-start.3
  115.6 53.4 %reduce-scatter.2.cloned.1.call-done = bf16[528,1024]{1,0:T(8,128)(2,1)} async-done(((bf16[528,4096]{1,0:T(8,128)(2,1)}), bf16[528,1024]{1,0:T(8,128)(2,1)}) %reduce-scatter.2.cloned.1.call-update) | async-done | bytes 1081360 | tf_op jit(solution)/shard_map/reduce_scatter | solution.py:431
  169.0 0.0 copy-start.1
  169.0 1.6 fusion
  170.7 8.9 %psum.7 = f32[528]{0:T(1024)S(1)} all-reduce(f32[528]{0:T(1024)S(1)} %fusion), channel_id=1, replica_groups=mesh['seq'=8,'tp'=4] {'tp'}, use_global_device_ids=true, to_apply=%region_2.3 | all-reduce | flops 528 | bytes 4224 | tf_op jit(solution)/shard_map/psum | solution.py:432
  179.6 0.0 copy-done.2
  179.6 0.0 copy-done.3
  179.6 0.0 copy-done.1
  179.6 0.5 fusion.3
  180.1 0.7 bitcast_dynamic-update-slice_fusion.7
  180.8 0.7 bitcast_dynamic-update-slice_fusion.6
  181.4 0.7 bitcast_dynamic-update-slice_fusion.5
  182.1 0.7 bitcast_dynamic-update-slice_fusion.4
  182.8 0.7 bitcast_dynamic-update-slice_fusion.3
  183.4 0.7 bitcast_dynamic-update-slice_fusion.2
  184.1 0.7 bitcast_dynamic-update-slice_fusion.1
  184.8 0.7 bitcast_dynamic-update-slice_fusion
  185.4 4.6 %all-to-all-start = ((bf16[8,64,1024]{2,1,0:T(8,128)(2,1)}), bf16[8,64,1024]{2,1,0:T(8,128)(2,1)S(1)}, u32[]{:S(2)}, u32[]{:S(2)}) async-start(bf16[8,64,1024]{2,1,0:T(8,128)(2,1)} %bitcast_dynamic-update-slice_fusion), calls=%async_computation.1 | async-start | bytes 2097152 | tf_op jit(solution)/shard_map/all_to_all | solution.py:438
  190.0 32.7 %all-gather = bf16[8,1,1024]{2,1,0:T(2,128)(2,1)S(1)} all-gather(bf16[1,1,1024]{2,1,0:T(2,128)(2,1)S(1)} %slice_bitcast_fusion), channel_id=1, replica_groups=mesh['seq'=8,'tp'=4] {'seq'}, dimensions={0}, use_global_device_ids=true | all-gather | bytes 18432 | tf_op jit(solution)/shard_map/all_gather | solution.py:439
  222.7 0.1 reduce
  222.8 0.6 copy.16
  223.4 0.0 all-to-all-done
  223.4 1.0 copy.25
  (9 shorter events, 0.1 us)
Async XLA Ops:
  7.2 0.7 copy-start
  7.2 161.9 %reduce-scatter.2.cloned.1.call-start = ((), (), s32[]{:S(2)}) async-start(), calls=%async_computation.2 | async-start | bytes 5406720 | tf_op jit(solution)/shard_map/reduce_scatter | solution.py:431
  115.6 64.0 %copy-start.2 = (bf16[528,1024]{1,0:T(8,128)(2,1)S(1)}, bf16[528,1024]{1,0:T(8,128)(2,1)}, u32[]{:S(2)}) copy-start(bf16[528,1024]{1,0:T(8,128)(2,1)} %get-tuple-element.5) | copy-start | bytes 3244036
  115.6 64.0 %copy-start.3 = (f32[1024]{0:T(1024)S(1)}, f32[1024]{0:T(1024)}, u32[]{:S(2)}) copy-start(f32[1024]{0:T(1024)} %param.14) | copy-start | bytes 12292
  169.0 10.6 %copy-start.1 = (bf16[528,1024]{1,0:T(8,128)(2,1)S(1)}, bf16[528,1024]{1,0:T(8,128)(2,1)}, u32[]{:S(2)}) copy-start(bf16[528,1024]{1,0:T(8,128)(2,1)} %reduce-scatter.2.cloned.1.call-done) | copy-start | bytes 3244036
  185.4 38.0 %all-to-all-start = ((bf16[8,64,1024]{2,1,0:T(8,128)(2,1)}), bf16[8,64,1024]{2,1,0:T(8,128)(2,1)S(1)}, u32[]{:S(2)}, u32[]{:S(2)}) async-start(bf16[8,64,1024]{2,1,0:T(8,128)(2,1)} %bitcast_dynamic-update-slice_fusion), calls=%async_computation.1 | async-start | bytes 2097152 | tf_op jit(solution)/shard_map/all_to_all | solution.py:438
Sparse Core Ops, SparseCore 0:
  115.7 53.2 reduce-scatter.1

commit v3 on v2

--- a/solution.py
+++ b/solution.py
@@ -385,6 +385,191 @@
     )(raw, value, cos, sin, qpos, kpos, qg, kg)
 
 
+def project_return(full, shards, piece, group, att, w, rows, gain, out, new, wv, d3, r3, s1, s2, r1, r2, p0, p1, p2, o, sq, sq_in, w_sem, l_sem, d_send, d_recv, m_send, m_recv, s_send, s_recv, z_send, z_recv, n_send, n_recv):
+    me, t = lax.axis_index("seq"), lax.axis_index("tp")
+    total, width = att.shape
+    count = total - PAD
+    prompt = me // group
+    near = [{"tp": t ^ j} for j in range(1, 4)]
+    loads = []
+    for j in range(4):
+        loads.append(pltpu.make_async_copy(w.at[:, pl.ds((t ^ j) * width, width)], wv.at[j], w_sem.at[j]))
+    for j in (3, 2, 1, 0):
+        loads[j].start()
+    greet([{"seq": me ^ k} for k in range(1, shards)] + near)
+    split = count // 2
+    side = ROWS // 2
+    spans = [(start, side, side) for start in range(split, count, ROWS)] + [(count, PAD, 0)]
+    late = len(spans)
+    spans += [(start, side, side) for start in range(split - ROWS, -1, -ROWS)]
+
+    def product(j, start, size, target):
+        def tile(i, carry):
+            col = pl.ds(pl.multiple_of(i * (width // 2), width // 2), width // 2)
+            part = jnp.dot(att[pl.ds(start, size), :], wv[j, :, col], preferred_element_type=jnp.float32)
+            target[pl.ds(start, size), col] = part.astype(target.dtype)
+            return carry
+
+        lax.fori_loop(0, 2, tile, 0)
+
+    def diagonal(i):
+        start, a, b = spans[i]
+        copies = [remote(d3.at[pl.ds(start, a)], r3.at[pl.ds(start, a)], d_send.at[0, i], d_recv.at[0, i], near[0])]
+        if b:
+            copies.append(
+                remote(d3.at[pl.ds(start + a, b)], r3.at[pl.ds(start + a, b)], d_send.at[1, i], d_recv.at[1, i], near[1])
+            )
+        return copies
+
+    def merged(i):
+        start, a, b = spans[i]
+        at = pl.ds(start, a + b)
+        return [
+            remote(s2.at[at], r2.at[at], m_send.at[1, i], m_recv.at[1, i], near[1]),
+            remote(s1.at[at], r1.at[at], m_send.at[0, i], m_recv.at[0, i], near[0]),
+        ]
+
+    def merge(i):
+        start, a, b = spans[i]
+        first, last = slice(start, start + a), slice(start + a, start + a + b)
+        copies, sums = diagonal(i), merged(i)
+        copies[0].wait_recv()
+        s2[first, :] = (p2[first, :] + r3[first, :].astype(jnp.float32)).astype(jnp.bfloat16)
+        if b:
+            s2[last, :] = p2[last, :].astype(jnp.bfloat16)
+        sums[0].start()
+        s1[first, :] = p1[first, :].astype(jnp.bfloat16)
+        if b:
+            copies[1].wait_recv()
+            s1[last, :] = (p1[last, :] + r3[last, :].astype(jnp.float32)).astype(jnp.bfloat16)
+        sums[1].start()
+
+    high = count - split + PAD
+    loads[3].wait()
+    product(3, split, high, d3)
+    for i in range(late):
+        for copy in diagonal(i):
+            copy.start()
+    product(3, 0, split, d3)
+    for i in range(late, len(spans)):
+        for copy in diagonal(i):
+            copy.start()
+    loads[2].wait()
+    product(2, split, high, p2)
+    loads[1].wait()
+    product(1, split, high, p1)
+    for i in range(late):
+        merge(i)
+    product(2, 0, split, p2)
+    product(1, 0, split, p1)
+    for i in range(late, len(spans)):
+        merge(i)
+    loads[0].wait()
+    product(0, split, high, p0)
+    product(0, 0, split, p0)
+
+    def squares(i):
+        return [remote(sq.at[i], sq_in.at[j, i], s_send.at[j, i], s_recv.at[j, i], near[j]) for j in range(3)]
+
+    def swap(k):
+        return remote(o.at[pl.ds(k * piece, piece)], out.at[me], z_send.at[k], z_recv.at[k], {"seq": me ^ k})
+
+    def fresh(m):
+        return remote(o.at[pl.ds(count, PAD)], new.at[prompt], n_send.at[m - 1], n_recv.at[m - 1], {"seq": me ^ (m * group)})
+
+    local = pltpu.make_async_copy(o.at[pl.ds(0, piece)], out.at[me], l_sem.at[0])
+    local_new = pltpu.make_async_copy(o.at[pl.ds(count, PAD)], new.at[prompt], l_sem.at[1])
+
+    def stage_one(i):
+        start, a, b = spans[i]
+        at = slice(start, start + a + b)
+        for copy in merged(i):
+            copy.wait_recv()
+        own = p0[at, :] + r1[at, :].astype(jnp.float32) + r2[at, :].astype(jnp.float32)
+        p0[at, :] = own
+        sq[i] = flat_tile(jnp.sum(lanes(own * own), -1, keepdims=True))
+        for copy in squares(i):
+            copy.start()
+
+    def stage_two(i):
+        start, a, b = spans[i]
+        at = slice(start, start + a + b)
+        for copy in squares(i):
+            copy.wait_recv()
+        flat = sq[i] + sq_in[0, i] + sq_in[1, i] + sq_in[2, i]
+        factor = lax.rsqrt(tall_tile(flat, a + b) / full + norm_eps)
+        for h in range(width // HD):
+            col = slice(h * HD, (h + 1) * HD)
+            o[at, col] = (
+                rows[at, col].astype(jnp.float32) + p0[at, col] * factor * gain[:, col]
+            ).astype(jnp.bfloat16)
+        if start == count:
+            local_new.start()
+            for m in range(1, shards // group):
+                fresh(m).start()
+        else:
+            for k in range(start // piece, (start + a + b) // piece):
+                if k == 0:
+                    local.start()
+                else:
+                    swap(k).start()
+
+    for i in range(len(spans)):
+        stage_one(i)
+        if i >= 1:
+            stage_two(i - 1)
+    stage_two(len(spans) - 1)
+    local.wait()
+    local_new.wait()
+    for k in range(1, shards):
+        swap(k).wait()
+    for m in range(1, shards // group):
+        fresh(m).wait()
+    for i in range(len(spans)):
+        for copy in diagonal(i) + merged(i) + squares(i):
+            copy.wait_send()
+
+
+def call_project(full, shards, piece, group, attention, w_out, rows, gain):
+    total, width = rows.shape
+    seqs = shards // group
+    tiles = (total - PAD) // ROWS + 1
+    dma = pltpu.SemaphoreType.DMA
+    half = pltpu.VMEM((total, width), jnp.bfloat16)
+    wide = pltpu.VMEM((total, width), jnp.float32)
+    return pl.pallas_call(
+        partial(project_return, full, shards, piece, group),
+        out_shape=(
+            jax.ShapeDtypeStruct((shards, piece, width), jnp.bfloat16),
+            jax.ShapeDtypeStruct((seqs, PAD, width), jnp.bfloat16),
+        ),
+        in_specs=[in_vmem(), pl.BlockSpec(memory_space=pl.ANY), in_vmem(), in_vmem()],
+        out_specs=(in_vmem(), in_vmem()),
+        scratch_shapes=[
+            pltpu.VMEM((4, width, width), jnp.bfloat16),
+            half, half, half, half, half, half,
+            wide, wide, wide,
+            half,
+            pltpu.VMEM((tiles, 8, ROWS), jnp.float32),
+            pltpu.VMEM((3, tiles, 8, ROWS), jnp.float32),
+            dma((4,)),
+            dma((2,)),
+            dma((2, tiles)),
+            dma((2, tiles)),
+            dma((2, tiles)),
+            dma((2, tiles)),
+            dma((3, tiles)),
+            dma((3, tiles)),
+            dma((shards,)),
+            dma((shards,)),
+            dma((seqs - 1,)),
+            dma((seqs - 1,)),
+        ],
+        compiler_params=pltpu.CompilerParams(collective_id=2, has_side_effects=True, vmem_limit_bytes=VMEM_LIMIT),
+        name="project_return",
+    )(attention, w_out, rows, gain)
+
+
 def fast_body(tokens, new_tokens, w_qkv, w_out, q_gain, k_gain, post_gain, lengths):
     seqs, pos_dev, width = tokens.shape
     full = w_qkv.shape[1]
@@ -417,28 +602,8 @@
     attention = call_attend(
         full, raw, value, cos, sin, query_pos[:, None], key_pos[None, :], q_gain[None], k_gain[None]
     )
-    return finish_fast(attention, w_out, rows, post_gain, full, seqs, pos_dev)
-
-
-def finish_fast(attention, w_out, rows, post_gain, full, seqs, pos_dev):
-    width = rows.shape[1]
-    shards = lax.axis_size("seq")
-    group = shards // seqs
-    piece = pos_dev // group
-    me = lax.axis_index("seq")
-    count = shards * piece
-    part = jnp.dot(attention, w_out, preferred_element_type=jnp.float32).astype(jnp.bfloat16)
-    own = lax.psum_scatter(part, "tp", scatter_dimension=1, tiled=True).astype(jnp.float32)
-    mean = lax.psum(jnp.sum(own * own, -1), "tp") / full
-    result = rows.astype(jnp.float32) + own * lax.rsqrt(mean[:, None] + norm_eps) * post_gain
-    result = result.astype(jnp.bfloat16)
-    blocks = jnp.stack(
-        [lax.dynamic_slice_in_dim(result, (me ^ k) * piece, piece, 0) for k in range(shards)]
-    )
-    out = lax.all_to_all(blocks, "seq", 0, 0, tiled=True)
-    new = lax.all_gather(result[count], "seq", axis=0)
-    new = new.reshape(seqs, group, width)[:, 0]
-    return out.reshape(seqs, pos_dev, width), new
+    out, new = call_project(full, shards, piece, group, attention, w_out, rows, post_gain[None])
+    return out.reshape(seqs, pos_dev, width), new[:, 0]
 
 
 def solution(mesh):

time: 232 us -> 174 us (0.75)
  Pallas kernels: 89.9 us -> 162 us
  waiting for transfers between devices: 53.4 us -> 0 us
  blocking collectives: 41.6 us -> 0 us
  between operations: 14.3 us -> 0.76 us
  matrix products: 10.4 us -> 0 us
  starting transfers between devices: 4.62 us -> 0 us
  local copies, waits for them, and re-layouts: 10.8 us -> 7.04 us
    pallas_call x0 -> x1, Pallas kernels: none -> 71.8 us  [call_project(): pl.pallas_call(partial(project_return, full, shards, piece, group), out_s...]
    reduce_scatter x1 -> x0, waiting for transfers between devices: 53.4 us -> none  [finish_fast(): lax.psum_scatter(part, 'tp', scatter_dimension=1, tiled=True)]
    all_gather x1 -> x0, blocking collectives: 32.7 us -> none  [finish_fast(): new = lax.all_gather(result[count], 'seq', axis=0)]
    dot_general x1 -> x0, matrix products: 10.4 us -> none  [finish_fast(): jnp.dot(attention, w_out, preferred_element_type=jnp.float32)]
    psum x1 -> x0, blocking collectives: 8.93 us -> none  [finish_fast(): mean = lax.psum(jnp.sum(own * own, -1), 'tp') / full]
    all_to_all x1 -> x0, starting transfers between devices: 4.58 us -> none  [finish_fast(): out = lax.all_to_all(blocks, 'seq', 0, 0, tiled=True)]
    unnamed x18 -> x4, local copies, waits for them, and re-layouts: 6.81 us -> 2.87 us
  transfers between devices with their start and end apart: 2 -> 0, of which waited for: 1 -> 0; matrix products, arithmetic and copies ran while one was open for 0% -> 0% of each run, Pallas kernels for 0% -> 0%
where the time goes in v3:
time: 174 us
  Pallas kernels  162 us (93%)
  local copies, waits for them, and re-layouts  7.04 us (4%)
  other arithmetic  4.05 us (2%)
    pallas_call x1, Pallas kernels, call_project(): pl.pallas_call(partial(project_return, full, shards, piece, group), out_s...  71.8 us
    pallas_call x1, Pallas kernels, call_gather(): pl.pallas_call(partial(gather_project, shards, piece), out_shape=(jax.Sha...  61.1 us
    pallas_call x1, Pallas kernels, call_attend(): pl.pallas_call(partial(attend, full), out_shape=jax.ShapeDtypeStruct((tot...  28.8 us

profile of v3, /device:TPU:0, one launch (start us, length us, event | category | flops | bytes accessed | tf_op | source)
XLA Modules:
  0.0 173.6 jit_solution(16467811320228725990)
XLA Ops:
  0.6 0.0 copy-start
  0.7 1.2 dynamic_slice.8
  1.9 0.7 fusion.18
  2.6 0.7 compare_select_fusion
  3.3 0.6 broadcast_in_dim.42.kpos
  3.9 0.0 copy-done
  3.9 0.6 pad.4.new
  4.6 0.8 broadcast_in_dim.46.qpos
  5.4 1.0 fusion
  6.4 0.8 pad_maximum_fusion.1.sin
  7.3 0.8 pad_maximum_fusion.cos
  8.1 61.1 %gather_project.1 = (bf16[528,1024]{1,0:T(8,128)(2,1)}, f32[2,528,1024]{2,1,0:T(8,128)}, bf16[528,1024]{1,0:T(8,128)(2,1)}) custom-call(bf16[8,64,1024]{2,1,0:T(8,128)(2,1)} %bitcast.9, bf16[16,1024]{1,0:T(8,128)(2,1)} %pad.4.new, bf16[3,4096,1024]{2,1,0:T(8,128)(2,1)} %w.2), custom_call_target="tpu_custom_call" | custom-call | tf_op jit(solution)/shard_map/gather_project/pallas_call | solution.py:333
  69.2 28.8 %attend.1.att = bf16[528,1024]{1,0:T(8,128)(2,1)} custom-call(f32[2,528,1024]{2,1,0:T(8,128)} %get-tuple-element.7.raw, bf16[528,1024]{1,0:T(8,128)(2,1)} %get-tuple-element.8.value, f32[528,128]{1,0:T(8,128)} %pad_maximum_fusion.cos, f32[528,128]{1,0:T(8,128)} %pad_maximum_fusion.1.sin, s32[528,1]{1,0:T(8,128)} %broadcast_in_dim.46.qpos, ...), custom_call_target="tpu_custom_call" | custom-call | tf_op jit(solution)/shard_map/attend/pallas_call | solution.py:365
  98.0 71.8 %project_return.1 = (bf16[8,64,1024]{2,1,0:T(8,128)(2,1)}, bf16[4,16,1024]{2,1,0:T(8,128)(2,1)}) custom-call(bf16[528,1024]{1,0:T(8,128)(2,1)} %attend.1.att, bf16[1024,4096]{1,0:T(8,128)(2,1)} %w.3, bf16[528,1024]{1,0:T(8,128)(2,1)} %get-tuple-element.9.rows, f32[1,1024]{1,0:T(1,128)} %bitcast.14), custom_call_target="tpu_custom_call" | custom-call | tf_op jit(solution)/shard_map/project_return/pallas_call | solution.py:540
  169.9 0.9 slice.3
  170.7 0.6 copy.13
  171.3 2.3 %copy.15 = bf16[4,128,1024]{2,1,0:T(8,128)(2,1)} copy(bf16[4,128,1024]{2,1,0:T(8,128)(2,1)} %bitcast.10) | data formatting | bytes 2097152
  (6 shorter events, 0.1 us)
Async XLA Ops:
  0.6 3.3 %copy-start = (bf16[4,1024]{1,0:T(4,128)(2,1)S(1)}, bf16[4,1024]{1,0:T(4,128)(2,1)}, u32[]{:S(2)}) copy-start(bf16[4,1024]{1,0:T(4,128)(2,1)} %param.9) | copy-start | bytes 24580

commit v4 on v3

--- a/solution.py
+++ b/solution.py
@@ -161,16 +161,24 @@
         return remote(at, x.at[j, pl.ds(count, PAD)], n_send.at[j - 1], n_recv.at[j - 1], near[j - 1])
 
     def multiply(j, start, size, clear):
-        def tile(i, carry):
-            c, col = i // 2, pl.ds(pl.multiple_of((i % 2) * (width // 2), width // 2), width // 2)
+        def tile(target, c, place, i):
+            col = pl.ds(pl.multiple_of(i * (width // 2), width // 2), width // 2)
             part = jnp.dot(x[j, pl.ds(start, size), :], wv[j, c, :, col], preferred_element_type=jnp.float32)
             if clear:
-                acc[c, pl.ds(start, size), col] = part
+                target[place, pl.ds(start, size), col] = part
             else:
-                acc[c, pl.ds(start, size), col] += part
+                target[place, pl.ds(start, size), col] += part
+
+        def scored(i, carry):
+            tile(raw, i // 2, i // 2, i % 2)
             return carry
 
-        lax.fori_loop(0, 6, tile, 0)
+        def valued(i, carry):
+            tile(acc, 2, 0, i)
+            return carry
+
+        lax.fori_loop(0, 4, scored, 0)
+        lax.fori_loop(0, 2, valued, 0)
 
     def arrive(k):
         if k == 0:
@@ -194,19 +202,18 @@
             fresh.wait()
             for j in range(1, 4):
                 tail(j).start()
-        if k >= 1:
+        if k >= 1 and k != middle:
             forward(k - 1)
-        if k == middle:
+        if k == middle - 1:
             loads[0].wait()
             multiply(0, 0, low, True)
-        if k == middle + 1:
+            forward(k)
             loads[1].wait()
             multiply(1, 0, low, False)
-        if k == middle + 2:
             loads[2].wait()
             multiply(2, 0, low, False)
+    multiply(0, low, high, True)
     forward(shards - 1)
-    multiply(0, low, high, True)
     loads[3].wait()
     for k in range(middle):
         second(1, k).wait_recv()
@@ -220,8 +227,7 @@
         second(1, k).wait_recv()
         second(2, k).wait_recv()
     multiply(3, low, high, False)
-    raw[...] = acc[0:2]
-    value[...] = acc[2].astype(jnp.bfloat16)
+    value[...] = acc[0].astype(jnp.bfloat16)
     rows[...] = x[0]
     for copy in swaps:
         copy.wait_send()
@@ -342,7 +348,7 @@
         scratch_shapes=[
             pltpu.VMEM((4, total, width), jnp.bfloat16),
             pltpu.VMEM((4, 3, width, width), jnp.bfloat16),
-            pltpu.VMEM((3, total, width), jnp.float32),
+            pltpu.VMEM((1, total, width), jnp.float32),
             dma((4,)),
             dma((2,)),
             dma((shards,)),
@@ -450,20 +456,18 @@
     for i in range(late):
         for copy in diagonal(i):
             copy.start()
-    product(3, 0, split, d3)
-    for i in range(late, len(spans)):
-        for copy in diagonal(i):
-            copy.start()
     loads[2].wait()
     product(2, split, high, p2)
     loads[1].wait()
     product(1, split, high, p1)
+    product(3, 0, split, d3)
     for i in range(late):
         merge(i)
+    for i in range(late, len(spans)):
+        for copy in diagonal(i):
+            copy.start()
     product(2, 0, split, p2)
     product(1, 0, split, p1)
-    for i in range(late, len(spans)):
-        merge(i)
     loads[0].wait()
     product(0, split, high, p0)
     product(0, 0, split, p0)
@@ -514,10 +518,17 @@
                 else:
                     swap(k).start()
 
-    for i in range(len(spans)):
+    for i in range(late - 1):
         stage_one(i)
-        if i >= 1:
-            stage_two(i - 1)
+    merge(late)
+    for i in range(late - 1):
+        stage_two(i)
+    for i in range(late + 1, len(spans)):
+        merge(i)
+    stage_one(late - 1)
+    for i in range(late, len(spans)):
+        stage_one(i)
+        stage_two(i - 1)
     stage_two(len(spans) - 1)
     local.wait()
     local_new.wait()

time: 174 us -> 165 us (0.948)
  Pallas kernels: 162 us -> 152 us
    pallas_call x1, Pallas kernels: 71.8 us -> 60.6 us  [call_project(): pl.pallas_call(partial(project_return, full, shards, piece, group), out_s...]
    pallas_call x1, Pallas kernels: 61.1 us -> 63 us  [call_gather(): pl.pallas_call(partial(gather_project, shards, piece), out_shape=(jax.Sha...]
where the time goes in v4:
time: 165 us; the launch traced here: 164 us
  Pallas kernels  152 us (92%)
  local copies, waits for them, and re-layouts  7.04 us (4%)
  other arithmetic  4.05 us (2%)
    pallas_call x1, Pallas kernels, call_gather(): pl.pallas_call(partial(gather_project, shards, piece), out_shape=(jax.Sha...  63 us
    pallas_call x1, Pallas kernels, call_project(): pl.pallas_call(partial(project_return, full, shards, piece, group), out_s...  60.6 us
    pallas_call x1, Pallas kernels, call_attend(): pl.pallas_call(partial(attend, full), out_shape=jax.ShapeDtypeStruct((tot...  28.8 us

profile of v4, /device:TPU:0, one launch (start us, length us, event | category | flops | bytes accessed | tf_op | source)
XLA Modules:
  0.0 164.2 jit_solution(4636609740943538067)
XLA Ops:
  0.6 0.0 copy-start
  0.7 1.2 dynamic_slice.8
  1.9 0.7 fusion.18
  2.6 0.7 compare_select_fusion
  3.3 0.6 broadcast_in_dim.42.kpos
  3.9 0.0 copy-done
  3.9 0.6 pad.4.new
  4.6 0.8 broadcast_in_dim.46.qpos
  5.4 1.0 fusion
  6.4 0.8 pad_maximum_fusion.1.sin
  7.3 0.8 pad_maximum_fusion.cos
  8.1 63.0 %gather_project.1 = (bf16[528,1024]{1,0:T(8,128)(2,1)}, f32[2,528,1024]{2,1,0:T(8,128)}, bf16[528,1024]{1,0:T(8,128)(2,1)}) custom-call(bf16[8,64,1024]{2,1,0:T(8,128)(2,1)} %bitcast.9, bf16[16,1024]{1,0:T(8,128)(2,1)} %pad.4.new, bf16[3,4096,1024]{2,1,0:T(8,128)(2,1)} %w.2), custom_call_target="tpu_custom_call" | custom-call | tf_op jit(solution)/shard_map/gather_project/pallas_call | solution.py:339
  71.1 28.8 %attend.1.att = bf16[528,1024]{1,0:T(8,128)(2,1)} custom-call(f32[2,528,1024]{2,1,0:T(8,128)} %get-tuple-element.7.raw, bf16[528,1024]{1,0:T(8,128)(2,1)} %get-tuple-element.8.value, f32[528,128]{1,0:T(8,128)} %pad_maximum_fusion.cos, f32[528,128]{1,0:T(8,128)} %pad_maximum_fusion.1.sin, s32[528,1]{1,0:T(8,128)} %broadcast_in_dim.46.qpos, ...), custom_call_target="tpu_custom_call" | custom-call | tf_op jit(solution)/shard_map/attend/pallas_call | solution.py:371
  99.9 60.6 %project_return.1 = (bf16[8,64,1024]{2,1,0:T(8,128)(2,1)}, bf16[4,16,1024]{2,1,0:T(8,128)(2,1)}) custom-call(bf16[528,1024]{1,0:T(8,128)(2,1)} %attend.1.att, bf16[1024,4096]{1,0:T(8,128)(2,1)} %w.3, bf16[528,1024]{1,0:T(8,128)(2,1)} %get-tuple-element.9.rows, f32[1,1024]{1,0:T(1,128)} %bitcast.14), custom_call_target="tpu_custom_call" | custom-call | tf_op jit(solution)/shard_map/project_return/pallas_call | solution.py:551
  160.5 0.9 slice.3
  161.4 0.6 copy.13
  162.0 2.3 %copy.15 = bf16[4,128,1024]{2,1,0:T(8,128)(2,1)} copy(bf16[4,128,1024]{2,1,0:T(8,128)(2,1)} %bitcast.10) | data formatting | bytes 2097152
  (6 shorter events, 0.1 us)
Async XLA Ops:
  0.6 3.3 %copy-start = (bf16[4,1024]{1,0:T(4,128)(2,1)S(1)}, bf16[4,1024]{1,0:T(4,128)(2,1)}, u32[]{:S(2)}) copy-start(bf16[4,1024]{1,0:T(4,128)(2,1)} %param.9) | copy-start | bytes 24580

commit v5 on v4

--- a/solution.py
+++ b/solution.py
@@ -315,13 +315,13 @@
             )
             scores = scores + bias[start : start + size, :]
             top = jnp.max(scores, -1, keepdims=True)
-            weights = jnp.exp((scores - top) * (HD ** (-0.5)))
+            weights = jnp.exp2((scores - top) * (HD ** (-0.5) * 1.4426950408889634))
             norm = jnp.sum(weights, -1, keepdims=True)
             mixed = jnp.dot(weights.astype(jnp.bfloat16), va[:, at], preferred_element_type=jnp.float32)
             out[start : start + size, at] = (mixed / norm).astype(jnp.bfloat16)
         return carry
 
-    lax.fori_loop(0, heads, one_head, 0)
+    lax.fori_loop(0, heads, one_head, 0, unroll=2)
     for copy in squares:
         copy.wait_send()
     send_v.wait_send()

time: 165 us -> 164 us (level)
  no operation moved by 1% of the time
where the time goes in v5:
time: 164 us; the launch traced here: 163 us
  Pallas kernels  151 us (92%)
  local copies, waits for them, and re-layouts  7.04 us (4%)
  other arithmetic  4.05 us (2%)
    pallas_call x1, Pallas kernels, call_gather(): pl.pallas_call(partial(gather_project, shards, piece), out_shape=(jax.Sha...  63 us
    pallas_call x1, Pallas kernels, call_project(): pl.pallas_call(partial(project_return, full, shards, piece, group), out_s...  60.6 us
    pallas_call x1, Pallas kernels, call_attend(): pl.pallas_call(partial(attend, full), out_shape=jax.ShapeDtypeStruct((tot...  27.8 us

profile of v5, /device:TPU:0, one launch (start us, length us, event | category | flops | bytes accessed | tf_op | source)
XLA Modules:
  0.0 163.2 jit_solution(17132458316898332033)
XLA Ops:
  0.6 0.0 copy-start
  0.7 1.2 dynamic_slice.8
  1.9 0.7 fusion.18
  2.6 0.7 compare_select_fusion
  3.3 0.6 broadcast_in_dim.42.kpos
  3.9 0.0 copy-done
  3.9 0.6 pad.4.new
  4.6 0.8 broadcast_in_dim.46.qpos
  5.4 1.0 fusion
  6.4 0.8 pad_maximum_fusion.1.sin
  7.3 0.8 pad_maximum_fusion.cos
  8.1 63.0 %gather_project.1 = (bf16[528,1024]{1,0:T(8,128)(2,1)}, f32[2,528,1024]{2,1,0:T(8,128)}, bf16[528,1024]{1,0:T(8,128)(2,1)}) custom-call(bf16[8,64,1024]{2,1,0:T(8,128)(2,1)} %bitcast.9, bf16[16,1024]{1,0:T(8,128)(2,1)} %pad.4.new, bf16[3,4096,1024]{2,1,0:T(8,128)(2,1)} %w.2), custom_call_target="tpu_custom_call" | custom-call | tf_op jit(solution)/shard_map/gather_project/pallas_call | solution.py:339
  71.1 27.8 %attend.1.att = bf16[528,1024]{1,0:T(8,128)(2,1)} custom-call(f32[2,528,1024]{2,1,0:T(8,128)} %get-tuple-element.7.raw, bf16[528,1024]{1,0:T(8,128)(2,1)} %get-tuple-element.8.value, f32[528,128]{1,0:T(8,128)} %pad_maximum_fusion.cos, f32[528,128]{1,0:T(8,128)} %pad_maximum_fusion.1.sin, s32[528,1]{1,0:T(8,128)} %broadcast_in_dim.46.qpos, ...), custom_call_target="tpu_custom_call" | custom-call | tf_op jit(solution)/shard_map/attend/pallas_call | solution.py:371
  98.9 60.6 %project_return.1 = (bf16[8,64,1024]{2,1,0:T(8,128)(2,1)}, bf16[4,16,1024]{2,1,0:T(8,128)(2,1)}) custom-call(bf16[528,1024]{1,0:T(8,128)(2,1)} %attend.1.att, bf16[1024,4096]{1,0:T(8,128)(2,1)} %w.3, bf16[528,1024]{1,0:T(8,128)(2,1)} %get-tuple-element.9.rows, f32[1,1024]{1,0:T(1,128)} %bitcast.14), custom_call_target="tpu_custom_call" | custom-call | tf_op jit(solution)/shard_map/project_return/pallas_call | solution.py:551
  159.5 0.9 slice.3
  160.3 0.6 copy.13
  160.9 2.3 %copy.15 = bf16[4,128,1024]{2,1,0:T(8,128)(2,1)} copy(bf16[4,128,1024]{2,1,0:T(8,128)(2,1)} %bitcast.10) | data formatting | bytes 2097152
  (6 shorter events, 0.1 us)
Async XLA Ops:
  0.6 3.3 %copy-start = (bf16[4,1024]{1,0:T(4,128)(2,1)S(1)}, bf16[4,1024]{1,0:T(4,128)(2,1)}, u32[]{:S(2)}) copy-start(bf16[4,1024]{1,0:T(4,128)(2,1)} %param.9) | copy-start | bytes 24580
